TPU v7x, 128 devices: a whole 4x4x4 slice. The times are simulated.
128 devices in a mesh: scen: 16 (over x, y), col: 8 (over z, core).
Axes of the slice: x: 4, y: 4, z: 4, core: 2. Of those that a mesh axis runs over, the one named last changes fastest.
Arguments:
- border: bfloat16 [64, 256, 2048], P('scen', None, 'col'), may hold values from -0.24077223 to 0.24077223
- touched: int32 [64, 8], replicated, may hold values from 0 to 63, as said below
- barrier: float32 [16384], replicated, may hold values from 0.5 to 8
Outputs:
- factored: float32 [16384, 16384], P('scen', 'col')
Inputs may be any that keep to these rules, and one draw needn't show every extreme that they name: Column blocks fall into 8 classes by their remainder modulo 8: touched[s, k] % 8 == k, so each scenario touches one block of each class.
All inputs are finite; a program needn't handle non-finite values.
Results may differ from a plain program's by a relative error of at most 0.0013.
Values may be sent and summed in bfloat16 or wider, within the bound.
A program may use at most 192 MiB of HBM per device.

v0:
```python
import jax
import jax.numpy as jnp
from jax import lax
from jax.sharding import PartitionSpec as P

N = 16384
TB = 256
KT = 8
PW = 1024


def from_root(block, axis, source):
    block = jnp.where(lax.axis_index(axis) == source, block, jnp.zeros_like(block))
    return lax.psum(block, axis)


def solve_right(corner, rows_block):
    return lax.linalg.triangular_solve(
        corner, rows_block, left_side=False, lower=True, transpose_a=True
    )


def per_device(border, touched, barrier):
    scen_count = lax.axis_size("scen")
    col_count = lax.axis_size("col")
    row_index = lax.axis_index("scen")
    col_index = lax.axis_index("col")
    local_rows = N // scen_count
    local_cols = N // col_count
    row_blocks = local_rows // TB
    col_blocks = local_cols // TB
    per_col = KT // col_count
    scenarios = border.shape[0]
    height = border.shape[1]
    complete = lax.all_gather(border, "col", axis=2, tiled=True)
    spread = complete.reshape(scenarios, height, per_col, col_count, TB)
    owned_cols = lax.dynamic_index_in_dim(spread, col_index, 3, keepdims=False)
    listing = touched.reshape(scen_count, scenarios, KT).transpose(1, 0, 2)
    class_pick = (jnp.arange(KT, dtype=jnp.int32) == row_index % KT).astype(jnp.int32)
    row_block = jnp.sum(listing * class_pick, axis=2)
    col_pick = (jnp.arange(col_count, dtype=jnp.int32) == col_index).astype(jnp.int32)
    col_block = jnp.sum(
        listing.reshape(scenarios, scen_count, per_col, col_count) * col_pick, axis=3
    )
    products = jnp.einsum(
        "sxk,sxm->skm",
        complete,
        owned_cols.reshape(scenarios, height, per_col * TB),
        preferred_element_type=jnp.float32,
    )
    products = products.reshape(scenarios, KT, TB, per_col * TB)
    outgoing = jnp.concatenate([products] * (scen_count // KT), axis=1)
    arrived = lax.all_to_all(outgoing, "scen", split_axis=1, concat_axis=1, tiled=True)
    contributions = arrived.reshape(scenarios, scen_count, TB, per_col, TB)
    row_hot = (
        row_block[:, :, None]
        == row_index + scen_count * jnp.arange(row_blocks, dtype=jnp.int32)[None, None, :]
    ).astype(jnp.float32)
    col_hot = (
        col_block[:, :, :, None] == col_index + col_count * jnp.arange(col_blocks, dtype=jnp.int32)
    ).astype(jnp.float32)
    weights = row_hot[:, :, None, :, None] * col_hot[:, :, :, None, :]
    summed = jnp.einsum(
        "jrtab,jritc->aibc", weights, contributions, precision=lax.Precision.HIGHEST
    )
    schur_block = summed.reshape(local_rows, local_cols)
    row_global = (
        (jnp.arange(row_blocks, dtype=jnp.int32)[:, None] * scen_count + row_index) * TB
        + jnp.arange(TB, dtype=jnp.int32)[None, :]
    ).reshape(-1)
    col_global = (
        (jnp.arange(col_blocks, dtype=jnp.int32)[:, None] * col_count + col_index) * TB
        + jnp.arange(TB, dtype=jnp.int32)[None, :]
    ).reshape(-1)
    diag_part = lax.dynamic_index_in_dim(
        barrier.reshape(row_blocks, scen_count, TB), row_index, 1, keepdims=False
    ).reshape(-1)
    schur_block = schur_block + jnp.where(
        row_global[:, None] == col_global[None, :], diag_part[:, None], 0.0
    )
    corner_blocks = PW // TB
    raw_rows = lax.all_gather(schur_block[:, :TB], "col", axis=1, tiled=True)[:, :PW]
    row_hot_corner = (jnp.arange(corner_blocks, dtype=jnp.int32) == row_index).astype(jnp.float32)
    col_hot_corner = (jnp.arange(corner_blocks, dtype=jnp.int32) == col_index).astype(jnp.float32)
    placed = (
        row_hot_corner[:, None, None, None]
        * schur_block[:TB, :TB][None, :, None, :]
        * col_hot_corner[None, None, :, None]
    )
    corner_full = lax.psum(placed, ("scen", "col")).reshape(PW, PW)
    corner = jnp.linalg.cholesky(corner_full)
    own_panel = solve_right(corner, raw_rows)
    received = []
    for parity in range(2):
        piece = from_root(
            own_panel.astype(jnp.bfloat16), "scen", col_index + col_count * parity
        ).astype(own_panel.dtype)
        received.append(piece.reshape(row_blocks, TB, PW))
    col_rows = jnp.stack(received, axis=1).reshape(local_cols, PW)
    lowered = schur_block - jnp.einsum(
        "rk,ck->rc", own_panel, col_rows, precision=lax.Precision.HIGHEST
    )
    first_col = jnp.minimum(col_index, corner_blocks - 1) * TB
    panel_here = lax.dynamic_slice_in_dim(own_panel, first_col, TB, 1)
    panel_wide = jnp.concatenate(
        [panel_here, jnp.zeros((local_rows, local_cols - TB), jnp.float32)], axis=1
    )
    result = jnp.where(
        col_global[None, :] < PW,
        panel_wide,
        jnp.where(row_global[:, None] >= PW, lowered, schur_block),
    )
    return result


def solution(mesh):
    in_specs = (P("scen", None, "col"), P(), P())
    out_specs = P("scen", "col")
    return jax.shard_map(
        per_device, mesh=mesh, in_specs=in_specs, out_specs=out_specs, check_vma=False
    )
```

profile of v0, /device:TPU:0, one launch (start us, length us, event | category | flops | bytes accessed | tf_op | source)
XLA Modules:
  0.0 1091.3 jit_solution(15312600759761212015)
XLA Ops:
  7.3 40.6 %all-gather.3.cloned.1.call-done = bf16[4,256,2048]{2,1,0:T(8,128)(2,1)} async-done(((bf16[4,256,256]{2,1,0:T(8,128)(2,1)}), bf16[4,256,2048]{2,1,0:T(8,128)(2,1)}) %all-gather.3.cloned.1.call-update) | async-done | bytes 4194320 | tf_op jit(solution)/shard_map/all_gather | solution.py:35
  53.2 6.8 convolution_bitcast_fusion
  60.1 9.9 copy.57
  69.9 15.7 %pad_maximum_fusion = f32[4,16,256,256]{3,0,2,1:T(4,128)} fusion(f32[4,8,256,256]{3,0,2,1:T(4,128)} %bitcast.147), kind=kLoop, calls=%fused_computation.2 | loop fusion | flops 4194304 | bytes 25165824 | tf_op jit(solution)/shard_map/concatenate | solution.py:52
  85.7 7.0 all-to-all-start
  94.3 295.9 %all-to-all-done = f32[4,16,256,256]{3,0,2,1:T(4,128)} async-done(((f32[4,16,256,256]{3,0,2,1:T(4,128)}), f32[4,16,256,256]{3,0,2,1:T(4,128)}, u32[]{:S(2)}, u32[]{:S(2)}) %all-to-all-start) | async-done | bytes 16777248 | tf_op jit(solution)/shard_map/all_to_all | solution.py:53
  390.1 24.1 %fusion.4 = f32[4,256,8,256]{3,2,0,1:T(8,128)} fusion(f32[4,16,256,256,1]{3,0,2,1,4:T(4,128)} %bitcast.2, f32[4,16,8]{1,2,0:T(8,128)S(1)} %compare_convert_fusion, f32[4,16,4]{1,0,2:T(4,128)S(1)} %compare_convert_fusion.1), kind=kOutput, calls=%fused_computation.14 | convolution fusion | flops 1610614784 | bytes 25168896 | tf_op jit(solution)/shard_map/jrtab,jritc->aibc/dot_general | solution.py:63
  414.2 9.3 copy.54
  423.5 5.5 copy.61
  439.7 155.8 %all-reduce.6.cloned.1.call-done = f32[1024,1024]{0,1:T(8,128)} async-done(((f32[1024,1024]{0,1:T(8,128)}), f32[1024,1024]{0,1:T(8,128)}) %all-reduce.6.cloned.1.call-update) | async-done | bytes 4194320 | tf_op jit(solution)/shard_map/psum | solution.py:90
  595.5 5.8 copy.30
  608.1 11.7 %cholesky.223 = f32[128,128]{1,0:T(8,128)S(1)} custom-call(f32[128,128]{1,0:T(8,128)S(1)} %cholesky.580), custom_call_target="Cholesky" | custom-call | tf_op jit(solution)/shard_map/jit(cholesky)/cholesky | solution.py:91
  619.8 9.8 custom-call.62
  636.1 11.9 %cholesky.244 = f32[128,128]{1,0:T(8,128)S(1)} custom-call(f32[128,128]{1,0:T(8,128)S(1)} %cholesky.584), custom_call_target="Cholesky" | custom-call | tf_op jit(solution)/shard_map/jit(cholesky)/cholesky | solution.py:91
  648.6 9.8 custom-call.63
  661.8 11.7 %cholesky.468 = f32[128,128]{1,0:T(8,128)S(1)} custom-call(f32[128,128]{1,0:T(8,128)S(1)} %cholesky.589), custom_call_target="Cholesky" | custom-call | tf_op jit(solution)/shard_map/jit(cholesky)/cholesky | solution.py:91
  674.1 9.8 custom-call.64
  687.5 11.9 %cholesky.487 = f32[128,128]{1,0:T(8,128)S(1)} custom-call(f32[128,128]{1,0:T(8,128)S(1)} %cholesky.594), custom_call_target="Cholesky" | custom-call | tf_op jit(solution)/shard_map/jit(cholesky)/cholesky | solution.py:91
  700.0 9.8 custom-call.65
  713.3 11.7 %cholesky.506 = f32[128,128]{1,0:T(8,128)S(1)} custom-call(f32[128,128]{1,0:T(8,128)S(1)} %cholesky.599), custom_call_target="Cholesky" | custom-call | tf_op jit(solution)/shard_map/jit(cholesky)/cholesky | solution.py:91
  725.7 10.2 custom-call.66
  739.2 11.7 %cholesky.526 = f32[128,128]{1,0:T(8,128)S(1)} custom-call(f32[128,128]{1,0:T(8,128)S(1)} %cholesky.604), custom_call_target="Cholesky" | custom-call | tf_op jit(solution)/shard_map/jit(cholesky)/cholesky | solution.py:91
  751.6 9.8 custom-call.67
  764.4 11.7 %cholesky.546 = f32[128,128]{1,0:T(8,128)S(1)} custom-call(f32[128,128]{1,0:T(8,128)S(1)} %cholesky.609), custom_call_target="Cholesky" | custom-call | tf_op jit(solution)/shard_map/jit(cholesky)/cholesky | solution.py:91
  776.7 9.8 custom-call.68
  789.1 11.7 %cholesky.564 = f32[128,128]{1,0:T(8,128)S(1)} custom-call(f32[128,128]{1,0:T(8,128)S(1)} %convolution_subtract_fusion.11), custom_call_target="Cholesky" | custom-call | tf_op jit(solution)/shard_map/jit(cholesky)/cholesky | solution.py:91
  811.0 4.8 select_select_fusion
  815.9 23.6 %while.1 = (s32[]{:T(128)}, f32[1024,1024]{1,0:T(8,128)}, s32[8,2]{0,1:T(2,128)S(1)}, f32[8,128,128]{2,1,0:T(8,128)S(1)}, s32[]{:T(128)}) while((s32[]{:T(128)}, f32[1024,1024]{1,0:T(8,128)}, s32[8,2]{0,1:T(2,128)S(1)}, f32[8,128,128]{2,1,0:T(8,128)S(1)}, s32[]{:T(128)}) %tuple.59), condition=%wide.while_cond, body=%wide.while_body.sunk | while | flops 2 | bytes 131189 | solution.py:18
  839.4 78.8 %custom-call.69 = f32[8,128,128]{1,2,0:T(8,128)S(1)} custom-call(f32[8,128,128]{2,1,0:T(8,128)S(1)} %get-tuple-element.12), custom_call_target="InvertDiagBlocksLowerTriangular" | custom-call | tf_op jit(solution)/shard_map/triangular_solve | solution.py:18
  953.2 100.3 %all-reduce.8.cloned.1.call-done = (bf16[4,1,256,1024]{3,2,1,0:T(8,128)(2,1)}, bf16[4,1,256,1024]{3,2,1,0:T(8,128)(2,1)}) async-done(((bf16[4,1,256,1024]{3,2,1,0:T(8,128)(2,1)}, bf16[4,1,256,1024]{3,2,1,0:T(8,128)(2,1)}), (bf16[4,1,256,1024]{3,2,1,0:T(8,128)(2,1)}, bf16[4,1,256,1024]{3,2,1,0:T(8,128)(2,1)})) %all-reduce.8.cloned.1.call-update) | async-done | bytes 4194320 | tf_op jit(solution)/shard_map/psum | solution.py:14
  1057.0 18.3 %fusion.2 = f32[1024,2048]{0,1:T(8,128)} fusion(f32[1024,2048]{0,1:T(8,128)} %copy-done, f32[1024,256]{0,1:T(8,128)S(1)} %constant_dynamic-slice_fusion.1, pred[2048]{0:T(1024)(128)(4,1)S(1)} %broadcast_compare_fusion, pred[1024]{0:T(1024)(128)(4,1)S(1)} %broadcast_compare_fusion.1, f32[1024,1024]{0,1:T(8,128)S(1)} %copy-done.3, ...), kind=kOutput, calls=%fused_computation.6 | convolution fusion | flops 25776095232 | bytes 26217472 | tf_op jit(solution)/shard_map/rk,ck->rc/dot_general | solution.py:100
  1075.2 9.1 copy.41
  (137 shorter events, 121.8 us)
Async XLA Ops:
  6.5 41.3 %all-gather.3.cloned.1.call-start = ((), (), s32[]{:S(2)}) async-start(), calls=%async_computation.1 | async-start | bytes 4718592 | tf_op jit(solution)/shard_map/all_gather | solution.py:35
  85.7 7.5 copy-start.5
  85.7 8.3 copy-start.4
  85.7 304.4 %all-to-all-start = ((f32[4,16,256,256]{3,0,2,1:T(4,128)}), f32[4,16,256,256]{3,0,2,1:T(4,128)}, u32[]{:S(2)}, u32[]{:S(2)}) async-start(f32[4,16,256,256]{3,0,2,1:T(4,128)} %pad_maximum_fusion), calls=%async_computation | async-start | bytes 33554432 | tf_op jit(solution)/shard_map/all_to_all | solution.py:53
  92.7 502.8 %all-reduce.6.cloned.1.call-start = ((), (), s32[]{:S(2)}) async-start(), calls=%async_computation.3 | async-start | bytes 8388608 | tf_op jit(solution)/shard_map/psum | solution.py:90
  430.0 3.4 copy-start
  437.2 481.1 %all-gather.5.cloned.1.call-start = ((), (), s32[]{:S(2)}) async-start(), calls=%async_computation.2 | async-start | bytes 9437184 | tf_op jit(solution)/shard_map/all_gather | solution.py:82
  439.6 613.9 %all-reduce.8.cloned.1.call-start = ((), (), s32[]{:S(2)}) async-start(), calls=%async_computation.4 | async-start | bytes 8388608 | tf_op jit(solution)/shard_map/psum | solution.py:14
  605.9 2.1 copy-start.1
  942.8 2.6 copy-start.2
  1053.5 3.4 copy-start.3
Sparse Core Ops, SparseCore 0:
  9.0 38.7 all-gather.2
  437.3 158.1 all-reduce.5
  597.2 48.2 all-gather.4
  952.0 101.4 all-reduce.7
where the time goes:
time: 1100 us; the launch traced here: 1090 us
  waiting for transfers between devices  593 us (54%)
  other arithmetic  284 us (26%)
  matrix products  96.7 us (9%)
  local copies, waits for them, and re-layouts  91.2 us (8%)
  between operations  18.7 us (2%)
    all_to_all x1, waiting for transfers between devices, per_device(): lax.all_to_all(outgoing, 'scen', split_axis=1, concat_axis=1, tiled=True)  296 us
    another operation x31, other arithmetic, per_device(): corner = jnp.linalg.cholesky(corner_full)  173 us
    psum x1, waiting for transfers between devices, per_device(): corner_full = lax.psum(placed, ('scen', 'col')).reshape(PW, PW)  156 us
    psum x1, waiting for transfers between devices, from_root(): return lax.psum(block, axis)  100 us
    another operation x3, other arithmetic, solve_right(): lax.linalg.triangular_solve(corner, rows_block, left_side=False, lower=Tr...  83.7 us
    all_gather x1, waiting for transfers between devices, per_device(): complete = lax.all_gather(border, 'col', axis=2, tiled=True)  40.6 us
    another operation x15, matrix products, solve_right(): lax.linalg.triangular_solve(corner, rows_block, left_side=False, lower=Tr...  24.4 us
    dot_general x1, matrix products, per_device(): jnp.einsum('jrtab,jritc->aibc', weights, contributions, precision=lax.Pre...  24.1 us
  transfers between devices with their start and end apart: 5, of which 4 were waited for; matrix products, arithmetic and copies ran while one was open for 29% of the time, Pallas kernels for 0%

commit v1 on v0

v1 whole, which is shorter than its diff:
```python
import jax
import jax.numpy as jnp
from jax import lax
from jax.experimental import pallas as pl
from jax.experimental.pallas import tpu as pltpu
from jax.sharding import PartitionSpec as P

N = 16384
TB = 256
KT = 8
PW = 1024
SCEN = 64
NB = 128
F32 = jnp.float32
BF16 = jnp.bfloat16
HIGHEST = lax.Precision.HIGHEST
MESH = pl.DeviceIdType.MESH
DMA = pltpu.SemaphoreType.DMA
NT = (((1,), (1,)), ((), ()))
TN = (((0,), (0,)), ((), ()))
MIB = 1024 * 1024

COMBOS = [
    (0, 0), (1, 0), (3, 0), (0, 1), (0, 3), (2, 0), (0, 2), (1, 1),
    (1, 3), (3, 1), (3, 3), (2, 1), (2, 3), (1, 2), (3, 2), (2, 2),
]


def plane_slots():
    slots = {}
    for e1, e2 in COMBOS:
        if e2 == 0:
            kinds = {0: (0, 1, 2, 3), 1: (0, 2, 3)}.get(e1, (2, 3))
        else:
            kinds = (2,) if e2 == 1 else ()
        for kind in kinds:
            slots[(e1, e2, kind)] = len(slots)
    return slots


SLOTS = plane_slots()


def rem4(v):
    return lax.rem(v + 8, 4)


def place():
    p = lax.axis_index("scen")
    q = lax.axis_index("col")
    return p, q, p // 4, lax.rem(p, 4), q // 2, lax.rem(q, 2)


def dev(x, y, z, c):
    return (x * 4 + y, z * 2 + c)


def remote(src, dst, send, recv, device):
    return pltpu.make_async_remote_copy(
        src_ref=src, dst_ref=dst, send_sem=send, recv_sem=recv,
        device_id=device, device_id_type=MESH,
    )


def greet(devices):
    bar = pltpu.get_barrier_semaphore()
    for d in devices:
        pl.semaphore_signal(bar, inc=1, device_id=d, device_id_type=MESH)
    pl.semaphore_wait(bar, len(devices))


def lane(v):
    return pl.multiple_of(v, 128)


class Plane:
    def __init__(self, own, tiles, send_sem, recv_sem):
        self.own, self.tiles = own, tiles
        self.send_sem, self.recv_sem = send_sem, recv_sem
        self.p, self.q, self.x, self.y, self.z, self.c = place()

    def geom(self, j):
        sy = j // 2
        return 1 - sy, sy, 1 - 2 * lax.rem(j, 2)

    def tile(self, e1, e2, j):
        sx, sy, d = self.geom(j)
        ox = rem4(self.x - d * (e1 * sx + e2 * sy))
        oy = rem4(self.y - d * (e1 * sy + e2 * sx))
        return 4 * (ox * 4 + oy) + j

    def event(self, e1, e2, extra=None):
        def body(j, _):
            sx, sy, d = self.geom(j)
            s = self.tile(e1, e2, j)
            dst = self.tiles(s)
            if (e1, e2) == (0, 0):
                src = self.own(j)
            else:
                src = dst
                remote(
                    src, src, self.send_sem.at[0],
                    self.recv_sem.at[(e1 * 4 + e2) * 4 + j], (self.p, self.q),
                ).wait_recv()

            def send(kind, first, sign, r1, r2):
                dx = (sx if first else sy) * d * sign
                dy = (sy if first else sx) * d * sign
                remote(
                    src, dst, self.send_sem.at[SLOTS[(e1, e2, kind)] * 4 + j],
                    self.recv_sem.at[(r1 * 4 + r2) * 4 + j],
                    dev(rem4(self.x + dx), rem4(self.y + dy), self.z, self.c),
                ).start()

            if e2 == 0:
                if e1 == 0:
                    send(0, True, 1, 1, 0)
                    send(1, True, -1, 3, 0)
                if e1 == 1:
                    send(0, True, 1, 2, 0)
                send(2, False, 1, e1, 1)
                send(3, False, -1, e1, 3)
            elif e2 == 1:
                send(2, False, 1, e1, 2)
            if extra is not None:
                extra(src, s, (e1 * 4 + e2) * 4 + j, d)
            return 0

        lax.fori_loop(0, 4, body, 0)

    def drain(self):
        t = self.tiles(0)

        def body(i, _):
            remote(t, t, self.send_sem.at[i], self.recv_sem.at[0], (self.p, self.q)).wait_send()
            return 0

        lax.fori_loop(0, 4 * len(SLOTS), body, 0)


def plane_peers():
    p, q, x, y, z, c = place()
    return [
        dev(rem4(x + 1), y, z, c), dev(rem4(x - 1), y, z, c),
        dev(x, rem4(y + 1), z, c), dev(x, rem4(y - 1), z, c),
    ]


def gather_kernel(b_ref, g_ref, h_ref, loc, ssem, rsem, zsem, psem, hsem):
    p, q, x, y, z, c = place()
    k = lax.rem(p, 8)
    zs, cs = k // 2, lax.rem(k, 2)
    here, partner = (p, q), dev(x, y, z, 1 - c)
    greet(plane_peers() + [dev(x, y, rem4(z + 1), c), dev(x, y, rem4(z - 1), c), partner])
    own = pltpu.make_async_copy(b_ref, g_ref.at[pl.ds(4 * p, 4)], loc)
    own.start()
    chain = c == cs
    source = jnp.logical_and(chain, z == zs)
    plane = Plane(lambda j: b_ref.at[j], lambda s: g_ref.at[s], ssem, rsem)

    def feed(src, s, h, d):
        @pl.when(source)
        def _():
            remote(src, h_ref.at[s], zsem.at[h], hsem.at[h], dev(x, y, rem4(z + d), c)).start()
            remote(src, h_ref.at[s], psem.at[h], hsem.at[h], partner).start()

    def relay(e1, e2, r):
        def body(j, _):
            d = 1 - 2 * lax.rem(j, 2)
            h = (e1 * 4 + e2) * 4 + j

            @pl.when(jnp.logical_and(chain, rem4((z - zs) * d) == r))
            def _():
                t = h_ref.at[plane.tile(e1, e2, j)]
                remote(t, t, zsem.at[0], hsem.at[h], here).wait_recv()
                if r < 3:
                    remote(t, t, zsem.at[h], hsem.at[h], dev(x, y, rem4(z + d), c)).start()
                remote(t, t, psem.at[h], hsem.at[h], partner).start()

            return 0

        lax.fori_loop(0, 4, body, 0)

    for n in range(len(COMBOS) + 3):
        if n < len(COMBOS):
            plane.event(*COMBOS[n], extra=feed)
        for r in (1, 2, 3):
            if 0 <= n - r < len(COMBOS):
                relay(*COMBOS[n - r], r)
    own.wait()
    plane.drain()
    t = g_ref.at[0]

    def last(i, _):
        d = 1 - 2 * lax.rem(i, 2)

        @pl.when(jnp.logical_and(chain, rem4((z - zs) * d) < 3))
        def _():
            remote(t, t, zsem.at[i], hsem.at[0], here).wait_send()

        @pl.when(chain)
        def _():
            remote(t, t, psem.at[i], hsem.at[0], here).wait_send()

        @pl.when(jnp.logical_not(chain))
        def _():
            remote(t, t, zsem.at[0], hsem.at[i], here).wait_recv()

        return 0

    lax.fori_loop(0, SCEN, last, 0)


def gather_borders(border):
    tiles = jax.ShapeDtypeStruct((SCEN, TB, TB), BF16)
    hbm = pl.BlockSpec(memory_space=pl.ANY)
    return pl.pallas_call(
        gather_kernel,
        out_shape=(tiles, tiles),
        in_specs=[hbm],
        out_specs=(hbm, hbm),
        scratch_shapes=[DMA(()), DMA((60,)), DMA((64,)), DMA((64,)), DMA((64,)), DMA((64,))],
        compiler_params=pltpu.CompilerParams(collective_id=0, has_side_effects=True),
        name="gather_borders",
    )(border)


PER_STEP = 4


def schur_kernel(touched_ref, g_ref, h_ref, bar_ref, out_ref):
    p, q = lax.axis_index("scen"), lax.axis_index("col")
    k = lax.rem(p, 8)
    step = pl.program_id(0)
    diagonal = k == q

    @pl.when(step == 0)
    def _():
        out_ref[...] = jnp.zeros_like(out_ref)

        @pl.when(diagonal)
        def _():
            eye = lax.broadcasted_iota(jnp.int32, (TB, TB), 0) == lax.broadcasted_iota(
                jnp.int32, (TB, TB), 1
            )
            for a in range(4):
                col = lane((2 * a + p // 8) * TB)
                row = bar_ref[pl.ds(a * 16 + p, 1), :]
                out_ref[a * TB:(a + 1) * TB, pl.ds(col, TB)] = jnp.where(eye, row, 0.0)

    for i in range(PER_STEP):
        s = step * PER_STEP + i
        big_row = touched_ref[s * KT + k]

        @pl.when(lax.rem(big_row, 16) == p)
        def _():
            row = pl.multiple_of((big_row // 16) * TB, TB)
            col = lane((touched_ref[s * KT + q] // 8) * TB)
            left = jnp.where(diagonal, g_ref[i], h_ref[i])
            out_ref[pl.ds(row, TB), pl.ds(col, TB)] += lax.dot_general(
                left, g_ref[i], TN, preferred_element_type=F32
            )


def assemble(touched, gathered, rows, barrier):
    block = pl.BlockSpec((PER_STEP, TB, TB), lambda i, t: (i, 0, 0))
    return pl.pallas_call(
        schur_kernel,
        out_shape=jax.ShapeDtypeStruct((1024, 2048), F32),
        grid_spec=pltpu.PrefetchScalarGridSpec(
            num_scalar_prefetch=1,
            grid=(SCEN // PER_STEP,),
            in_specs=[block, block, pl.BlockSpec((N // TB, TB), lambda i, t: (0, 0))],
            out_specs=pl.BlockSpec((1024, 2048), lambda i, t: (0, 0)),
        ),
        compiler_params=pltpu.CompilerParams(vmem_limit_bytes=48 * MIB),
        name="assemble",
    )(touched.reshape(-1), gathered, rows, barrier.reshape(N // TB, TB))


def spread_kernel(s_ref, pk_ref, raw_ref, st_ref, loc, ssend, srecv, zsend, zrecv,
                  xsend, xrecv, csend, crecv, asend, arecv):
    p, q, x, y, z, c = place()
    here, partner = (p, q), dev(x, y, z, 1 - c)
    greet([(lax.rem(p + i, 16), q) for i in range(1, 16)]
          + [(p, lax.rem(q + i, 8)) for i in range(1, 8)])
    holds = q < 4
    corner = jnp.logical_and(holds, jnp.logical_and(p < 4, p >= q))

    def cols(k, m):
        return pl.ds(lane((k * (k + 1) // 2 + m) * TB), TB)

    def scatter(i, wait):
        g = lax.rem(p + i, 16)
        cp = remote(s_ref.at[pl.ds(2 * g, 2), :, pl.ds(0, TB)], st_ref.at[p],
                    ssend.at[i - 1], srecv.at[p], (g, q))
        cp.wait_send() if wait else cp.start()

    own_tile = pltpu.make_async_copy(
        s_ref.at[pl.ds(2 * p, 2), :, pl.ds(0, TB)], st_ref.at[lax.rem(p, 4)], loc.at[0])

    @pl.when(corner)
    def _():
        for i in range(1, 16):
            scatter(i, False)
        own_tile.start()

    def rows_to(i):
        to = lax.rem(q + i, 8)
        return remote(s_ref.at[pl.ds(16 * to, 16), :, pl.ds(0, TB)],
                      raw_ref.at[:, :, pl.ds(lane(lax.rem(q, 4) * TB), TB)],
                      asend.at[i - 1], arecv.at[lax.rem(q, 4)], (p, to))

    own_rows = pltpu.make_async_copy(
        s_ref.at[pl.ds(16 * q, 16), :, pl.ds(0, TB)],
        raw_ref.at[:, :, pl.ds(lane(lax.rem(q, 4) * TB), TB)], loc.at[1])

    @pl.when(holds)
    def _():
        for i in range(1, 8):
            rows_to(i).start()
        own_rows.start()

    def fan(k, i):
        to = lax.rem(q + i, 8)
        half = lax.rem(to, 2)
        m = lax.rem(q, 4)
        return remote(st_ref.at[k, half], pk_ref.at[p, half, :, cols(k, m)],
                      zsend.at[k * 7 + i - 1], zrecv.at[k * 4 + m], (p, to))

    def keep(k):
        return pltpu.make_async_copy(
            st_ref.at[k, c], pk_ref.at[p, c, :, cols(k, lax.rem(q, 4))], loc.at[2 + k])

    for k in range(4):
        @pl.when(q <= k)
        def _():
            @pl.when(p == k)
            def _():
                own_tile.wait()

            @pl.when(p != k)
            def _():
                remote(st_ref.at[k], st_ref.at[k], ssend.at[0], srecv.at[k], here).wait_recv()

            for i in range(1, 8):
                fan(k, i).start()
            keep(k).start()

    for k in range(4):
        for m in range(k + 1):
            @pl.when(q == m)
            def _():
                keep(k).wait()

            @pl.when(q != m)
            def _():
                t = pk_ref.at[p, c, :, cols(k, m)]
                remote(t, t, zsend.at[0], zrecv.at[k * 4 + m], here).wait_recv()

    def shard(i):
        return remote(pk_ref.at[p, c], pk_ref.at[p, c], xsend.at[i - 1], xrecv.at[i - 1],
                      (lax.rem(p + i, 16), q))

    for i in range(1, 16):
        shard(i).start()
    for i in range(1, 16):
        t = pk_ref.at[lax.rem(p + 16 - i, 16), c]
        remote(t, t, xsend.at[i - 1], xrecv.at[i - 1], here).wait_recv()
    swap = remote(pk_ref.at[:, c], pk_ref.at[:, c], csend, crecv, partner)
    swap.start()

    for i in range(1, 16):
        shard(i).wait_send()

    @pl.when(corner)
    def _():
        for i in range(1, 16):
            scatter(i, True)

    @pl.when(holds)
    def _():
        for i in range(1, 8):
            rows_to(i).wait_send()
        own_rows.wait()

    for k in range(4):
        @pl.when(q <= k)
        def _():
            for i in range(1, 8):
                fan(k, i).wait_send()

    for m in range(4):
        @pl.when(q != m)
        def _():
            t = raw_ref.at[:, :, pl.ds(m * TB, TB)]
            remote(t, t, asend.at[0], arecv.at[m], here).wait_recv()

    swap.wait_send()
    t = pk_ref.at[:, 1 - c]
    remote(t, t, csend, crecv, here).wait_recv()


def spread(schur):
    hbm = pl.BlockSpec(memory_space=pl.ANY)
    return pl.pallas_call(
        spread_kernel,
        out_shape=(
            jax.ShapeDtypeStruct((16, 2, 8, 2560), F32),
            jax.ShapeDtypeStruct((16, 8, PW), F32),
        ),
        in_specs=[hbm],
        out_specs=(hbm, hbm),
        scratch_shapes=[
            pltpu.VMEM((4, 2, 8, TB), F32), DMA((6,)), DMA((15,)), DMA((4,)), DMA((28,)),
            DMA((16,)), DMA((15,)), DMA((15,)), DMA(()), DMA(()), DMA((7,)), DMA((4,)),
        ],
        compiler_params=pltpu.CompilerParams(collective_id=1, has_side_effects=True),
        name="spread_corner",
    )(schur.reshape(128, 8, 2048))


def pair_step(a0, b, d, r0, r1, g0, g1):
    det = a0 * d - b * b
    inv = 1.0 / det
    q0 = lax.rsqrt(a0)
    q1 = lax.rsqrt(a0 * det)
    ci, bi, ai = d * inv, b * inv, a0 * inv
    x0, x1 = g0 * q0, (a0 * g1 - b * g0) * q1
    z0, z1 = ci * r0 - bi * r1, ai * r1 - bi * r0
    m0, m1 = ci * g0 - bi * g1, ai * g1 - bi * g0
    return x0, x1, z0, z1, m0, m1, ci, bi, ai


def four_columns(a, m, o):
    c = [jnp.broadcast_to(a[:, o + t:o + t + 1], (NB, NB)) for t in range(4)]
    r = [a[o + t:o + t + 1, :] for t in range(4)]
    g = [m[o + t:o + t + 1, :] for t in range(4)]
    w = [[c[u][o + t:o + t + 1, :] for u in range(t + 1)] for t in range(4)]
    x0, x1, z0, z1, m0, m1, ci, bi, ai = pair_step(
        w[0][0], w[1][0], w[1][1], r[0], r[1], g[0], g[1])
    z02, z12 = ci * w[2][0] - bi * w[2][1], ai * w[2][1] - bi * w[2][0]
    z03, z13 = ci * w[3][0] - bi * w[3][1], ai * w[3][1] - bi * w[3][0]
    w22 = w[2][2] - w[2][0] * z02 - w[2][1] * z12
    w32 = w[3][2] - w[3][0] * z02 - w[3][1] * z12
    w33 = w[3][3] - w[3][0] * z03 - w[3][1] * z13
    r2 = r[2] - w[2][0] * z0 - w[2][1] * z1
    r3 = r[3] - w[3][0] * z0 - w[3][1] * z1
    g2 = g[2] - w[2][0] * m0 - w[2][1] * m1
    g3 = g[3] - w[3][0] * m0 - w[3][1] * m1
    x2, x3, z2, z3, m2, m3, _, _, _ = pair_step(w22, w32, w33, r2, r3, g2, g3)
    zt0, zt1 = z0 - z02 * z2 - z03 * z3, z1 - z12 * z2 - z13 * z3
    mt0, mt1 = m0 - z02 * m2 - z03 * m3, m1 - z12 * m2 - z13 * m3
    a = a - c[0] * zt0 - c[1] * zt1 - (c[2] * z2 + c[3] * z3)
    m = m - c[0] * mt0 - c[1] * mt1 - (c[2] * m2 + c[3] * m3)
    return a, m, [x0, x1, x2, x3]


def invert_factor(a, out_ref):
    eye = (
        lax.broadcasted_iota(jnp.int32, (NB, NB), 0)
        == lax.broadcasted_iota(jnp.int32, (NB, NB), 1)
    ).astype(F32)

    def body(it, carry):
        a, m = carry
        rows = []
        for o in range(0, 16, 4):
            a, m, x = four_columns(a, m, o)
            rows += x
        out_ref[pl.ds(pl.multiple_of(it * 16, 16), 16), :] = jnp.concatenate(rows, 0)
        a = pltpu.roll(a, NB - 16, 1)
        return jnp.concatenate([a[16:], a[:16]], 0), jnp.concatenate([m[16:], m[:16]], 0)

    lax.fori_loop(0, NB // 16, body, (a, eye))


def factor_kernel(pk_ref, raw_ref, pf_ref, pb_ref, a_ref, x_ref):
    end = PW + NB
    for k in range(4):
        width = TB * (k + 1)
        first = TB * (k * (k + 1) // 2)
        a_ref[TB * k:TB * (k + 1), 0:width] = pk_ref[:, first:first + width]
    a_ref[PW:end, :] = raw_ref[...]
    for n in range(PW // NB):
        lo, hi = NB * n, NB * (n + 1)
        invert_factor(a_ref[lo:hi, lo:hi], x_ref)
        a_ref[hi:end, lo:hi] = lax.dot_general(
            a_ref[hi:end, lo:hi], x_ref[...], NT, precision=HIGHEST, preferred_element_type=F32)
        for j in range(n + 1, PW // NB):
            jl, jh = NB * j, NB * (j + 1)
            a_ref[jl:end, jl:jh] -= lax.dot_general(
                a_ref[jl:end, lo:hi], a_ref[jl:jh, lo:hi], NT,
                precision=HIGHEST, preferred_element_type=F32)
    solved = a_ref[PW:end, :]
    pf_ref[...] = solved
    pb_ref[...] = solved.astype(BF16)


def factor(packed, raw):
    return pl.pallas_call(
        factor_kernel,
        out_shape=(
            jax.ShapeDtypeStruct((NB, PW), F32), jax.ShapeDtypeStruct((NB, PW), BF16)),
        scratch_shapes=[pltpu.VMEM((PW + NB, PW), F32), pltpu.VMEM((NB, NB), F32)],
        compiler_params=pltpu.CompilerParams(vmem_limit_bytes=48 * MIB),
        name="factor_corner",
    )(packed.reshape(TB, 2560), raw.reshape(NB, PW))


def exchange_kernel(pf_ref, pb_ref, pc_ref, pr_ref, pan_ref, loc, wsend, wrecv, ssem, rsem,
                    zsend, zrecv, csend, crecv, fsend, frecv):
    p, q, x, y, z, c = place()
    here, partner = (p, q), dev(x, y, z, 1 - c)
    twin = (8 * (p // 8) + q, lax.rem(p, 8))
    alone = lax.rem(p, 8) == q
    bar = pltpu.get_barrier_semaphore()
    for d in plane_peers() + [(p, lax.rem(q + i, 8)) for i in range(1, 8)]:
        pl.semaphore_signal(bar, inc=1, device_id=d, device_id_type=MESH)

    @pl.when(alone)
    def _():
        pl.semaphore_wait(bar, 11)

    @pl.when(jnp.logical_not(alone))
    def _():
        pl.semaphore_signal(bar, inc=1, device_id=twin, device_id_type=MESH)
        pl.semaphore_wait(bar, 12)
        remote(pb_ref, pc_ref.at[twin[0]], wsend, wrecv, twin).start()

    mine = pltpu.make_async_copy(pb_ref, pc_ref.at[p], loc.at[0])

    @pl.when(alone)
    def _():
        mine.start()

    keep = pltpu.make_async_copy(pb_ref, pr_ref.at[q], loc.at[1])
    keep.start()

    def over(i):
        return remote(pb_ref, pr_ref.at[q], zsend.at[i - 1], zrecv.at[i - 1],
                      dev(x, y, rem4(z + i), c))

    def across(i):
        src = pb_ref if i == 0 else pr_ref.at[2 * rem4(z - i) + c]
        return remote(src, pr_ref.at[2 * rem4(z - i) + c], csend.at[i], crecv.at[i], partner)

    def block(m):
        return remote(pf_ref.at[:, :, pl.ds(m * TB, TB)], pan_ref.at[q],
                      fsend.at[m], frecv.at[q], (p, m))

    def block_here(m):
        return pltpu.make_async_copy(
            pf_ref.at[:, :, pl.ds(m * TB, TB)], pan_ref.at[q], loc.at[2])

    for i in (1, 3, 2):
        over(i).start()
    across(0).start()
    for m in range(4):
        @pl.when(q != m)
        def _():
            block(m).start()

        @pl.when(q == m)
        def _():
            block_here(m).start()

    plane = Plane(lambda j: pc_ref.at[p, j], lambda s: pc_ref.at[s // 4, lax.rem(s, 4)], ssem, rsem)

    @pl.when(alone)
    def _():
        mine.wait()

    @pl.when(jnp.logical_not(alone))
    def _():
        remote(pb_ref, pc_ref.at[p], wsend, wrecv, twin).wait_recv()

    for n in range(len(COMBOS)):
        plane.event(*COMBOS[n])
        if n in (2, 4, 6):
            i = {2: 1, 4: 3, 6: 2}[n]
            t = pr_ref.at[2 * rem4(z - i) + c]
            remote(t, t, zsend.at[0], zrecv.at[i - 1], here).wait_recv()
            across(i).start()
    plane.drain()
    keep.wait()
    for i in (1, 2, 3):
        over(i).wait_send()
    for i in range(4):
        across(i).wait_send()
        t = pr_ref.at[2 * rem4(z - i) + 1 - c]
        remote(t, t, csend.at[0], crecv.at[i], here).wait_recv()
    for m in range(4):
        @pl.when(q != m)
        def _():
            block(m).wait_send()

        @pl.when(q == m)
        def _():
            block_here(m).wait()
            for i in range(1, 8):
                t = pan_ref.at[lax.rem(q + i, 8)]
                remote(t, t, fsend.at[0], frecv.at[lax.rem(q + i, 8)], here).wait_recv()

    @pl.when(jnp.logical_not(alone))
    def _():
        remote(pb_ref, pc_ref.at[p], wsend, wrecv, twin).wait_send()


def exchange(pf, pb):
    hbm = pl.BlockSpec(memory_space=pl.ANY)
    return pl.pallas_call(
        exchange_kernel,
        out_shape=(
            jax.ShapeDtypeStruct((16, 4, 32, PW), BF16),
            jax.ShapeDtypeStruct((8, 4, 32, PW), BF16),
            jax.ShapeDtypeStruct((8, 16, 8, TB), F32),
        ),
        in_specs=[hbm, hbm],
        out_specs=(hbm, hbm, hbm),
        scratch_shapes=[
            DMA((3,)), DMA(()), DMA(()), DMA((60,)), DMA((64,)), DMA((3,)), DMA((3,)),
            DMA((4,)), DMA((4,)), DMA((4,)), DMA((8,)),
        ],
        compiler_params=pltpu.CompilerParams(collective_id=2, has_side_effects=True),
        name="exchange_panel",
    )(pf.reshape(16, 8, PW), pb.reshape(4, 32, PW))


STRIP = 128


def update_kernel(s_ref, pr_ref, pc_ref, pan_ref, out_ref):
    p, q = lax.axis_index("scen"), lax.axis_index("col")
    a = pl.program_id(0) // (TB // STRIP)
    low = jnp.logical_or(a > 0, p >= 4)
    panel = q < 4
    for b in range(8):
        cols = slice(b * TB, (b + 1) * TB)
        first = (b % 2) * 1024 + (b // 2) * TB

        def lowered():
            out_ref[:, cols] = s_ref[:, cols] - lax.dot_general(
                pr_ref[...], pc_ref[first:first + TB, :], NT, preferred_element_type=F32)

        def kept():
            out_ref[:, cols] = s_ref[:, cols]

        def solved():
            out_ref[:, cols] = pan_ref[...]

        if b == 0:
            pl.when(panel)(solved)
            pl.when(jnp.logical_and(jnp.logical_not(panel), low))(lowered)
            pl.when(jnp.logical_and(jnp.logical_not(panel), jnp.logical_not(low)))(kept)
        else:
            pl.when(low)(lowered)
            pl.when(jnp.logical_not(low))(kept)


def update(schur, rows, cols, panel):
    strip = pl.BlockSpec((STRIP, 2048), lambda i: (i, 0))
    return pl.pallas_call(
        update_kernel,
        out_shape=jax.ShapeDtypeStruct((1024, 2048), F32),
        grid=(1024 // STRIP,),
        in_specs=[
            strip,
            pl.BlockSpec((STRIP, PW), lambda i: (i, 0)),
            pl.BlockSpec((2048, PW), lambda i: (0, 0)),
            pl.BlockSpec((STRIP, TB), lambda i: (i, 0)),
        ],
        out_specs=strip,
        compiler_params=pltpu.CompilerParams(vmem_limit_bytes=48 * MIB),
        name="update",
    )(schur, rows.reshape(1024, PW), cols.reshape(2048, PW), panel.reshape(1024, TB))


def per_device(border, touched, barrier):
    gathered, rows = gather_borders(border)
    schur = assemble(touched, gathered, rows, barrier)
    packed, raw = spread(schur)
    solved, rounded = factor(packed, raw)
    panel_cols, panel_rows, panel = exchange(solved, rounded)
    return update(schur, panel_rows, panel_cols, panel)


def solution(mesh):
    in_specs = (P("scen", None, "col"), P(), P())
    out_specs = P("scen", "col")
    return jax.shard_map(
        per_device, mesh=mesh, in_specs=in_specs, out_specs=out_specs, check_vma=False
    )
```

time: 1100 us -> 283 us (0.26)
  waiting for transfers between devices: 593 us -> 0 us
  other arithmetic: 284 us -> 0 us
  Pallas kernels: 0 us -> 272 us
  matrix products: 96.7 us -> 0 us
  local copies, waits for them, and re-layouts: 91.2 us -> 8.8 us
  between operations: 18.7 us -> 0.07 us
    all_to_all x1 -> x0, waiting for transfers between devices: 296 us -> none  [per_device(): lax.all_to_all(outgoing, 'scen', split_axis=1, concat_axis=1, tiled=True)]
    pallas_call x0 -> x6, Pallas kernels: none -> 272 us  [the longest x1 70 us: gather_borders(): pl.pallas_call(gather_kernel, out_shape=(tiles, tiles), in_specs=[hbm], o...]
    another operation x35 -> x0, other arithmetic: 259 us -> none  [the longest x31 173 us: per_device(): corner = jnp.linalg.cholesky(corner_full)]
    psum x2 -> x0, waiting for transfers between devices: 256 us -> none  [the longest x1 156 us: per_device(): corner_full = lax.psum(placed, ('scen', 'col')).reshape(PW, PW)]
    dot_general x3 -> x0, matrix products: 49.2 us -> none  [the longest x1 24.1 us: per_device(): jnp.einsum('jrtab,jritc->aibc', weights, contributions, precision=lax.Pre...]
    another operation x29 -> x0, matrix products: 47.5 us -> none  [the longest x15 24.4 us: solve_right(): lax.linalg.triangular_solve(corner, rows_block, left_side=False, lower=Tr...]
    all_gather x2 -> x0, waiting for transfers between devices: 40.6 us -> none  [the longest x1 40.6 us: per_device(): complete = lax.all_gather(border, 'col', axis=2, tiled=True)]
    another operation x35 -> x0, local copies, waits for them, and re-layouts: 32.5 us -> none
  transfers between devices with their start and end apart: 5 -> 0, of which waited for: 4 -> 0; matrix products, arithmetic and copies ran while one was open for 29% -> 0% of each run, Pallas kernels for 0% -> 0%
where the time goes in v1:
time: 283 us; the launch traced here: 281 us
  Pallas kernels  272 us (96%)
  local copies, waits for them, and re-layouts  8.8 us (3%)
    pallas_call x1, Pallas kernels, gather_borders(): pl.pallas_call(gather_kernel, out_shape=(tiles, tiles), in_specs=[hbm], o...  70 us
    pallas_call x1, Pallas kernels, spread(): pl.pallas_call(spread_kernel, out_shape=(jax.ShapeDtypeStruct((16, 2, 8,...  60.3 us
    pallas_call x1, Pallas kernels, factor(): pl.pallas_call(factor_kernel, out_shape=(jax.ShapeDtypeStruct((NB, PW), F...  58.8 us
    pallas_call x1, Pallas kernels, exchange(): pl.pallas_call(exchange_kernel, out_shape=(jax.ShapeDtypeStruct((16, 4, 3...  49.2 us
    pallas_call x1, Pallas kernels, assemble(): pl.pallas_call(schur_kernel, out_shape=jax.ShapeDtypeStruct((1024, 2048),...  19.3 us
    pallas_call x1, Pallas kernels, update(): pl.pallas_call(update_kernel, out_shape=jax.ShapeDtypeStruct((1024, 2048)...  14.3 us
    unnamed x13, local copies, waits for them, and re-layouts  7.84 us

profile of v1, /device:TPU:0, one launch (start us, length us, event | category | flops | bytes accessed | tf_op | source)
XLA Modules:
  0.0 280.8 jit_solution(5922374921357732172)
XLA Ops:
  0.0 0.8 copy.4
  0.8 0.1 reshape.30.touched_ref
  0.9 0.9 reshape.31.bar_ref
  1.7 70.0 %gather_borders.1 = (bf16[64,256,256]{2,1,0:T(8,128)(2,1)}, bf16[64,256,256]{2,1,0:T(8,128)(2,1)}) custom-call(bf16[4,256,256]{2,1,0:T(8,128)(2,1)} %b_ref.1), custom_call_target="tpu_custom_call" | custom-call | tf_op jit(solution)/shard_map/gather_borders/pallas_call | solution.py:217
  71.7 19.3 %assemble.1.s_ref = f32[1024,2048]{1,0:T(8,128)} custom-call(s32[512]{0:T(512)S(1)} %reshape.30.touched_ref, bf16[64,256,256]{2,1,0:T(8,128)(2,1)} %get-tuple-element.14.g_ref, bf16[64,256,256]{2,1,0:T(8,128)(2,1)} %get-tuple-element.15.h_ref, f32[64,256]{1,0:T(8,128)S(1)} %reshape.31.bar_ref), custom_call_target="tpu_custom_call" | custom-call | tf_op jit(solution)/shard_map/assemble/pallas_call | solution.py:267
  91.0 60.3 %spread_corner.1 = (f32[16,2,8,2560]{3,2,1,0:T(8,128)}, f32[16,8,1024]{2,1,0:T(8,128)}) custom-call(f32[128,8,2048]{2,1,0:T(8,128)} %bitcast.14), custom_call_target="tpu_custom_call" | custom-call | tf_op jit(solution)/shard_map/spread_corner/pallas_call | solution.py:406
  151.3 0.0 copy-start
  151.4 1.7 copy-done
  153.1 0.0 copy-start.4
  153.1 1.0 copy-done.4
  154.1 58.8 %factor_corner.1 = (f32[128,1024]{1,0:T(8,128)S(1)}, bf16[128,1024]{1,0:T(8,128)(2,1)S(1)}) custom-call(f32[256,2560]{1,0:T(8,128)S(1)} %bitcast.8, f32[128,1024]{1,0:T(8,128)S(1)} %bitcast.12), custom_call_target="tpu_custom_call" | custom-call | tf_op jit(solution)/shard_map/factor_corner/pallas_call | solution.py:501
  213.0 0.0 copy-start.3
  213.0 0.8 copy-done.3
  213.8 0.0 copy-start.5
  213.8 0.7 copy-done.5
  214.5 49.2 %exchange_panel.1 = (bf16[16,4,32,1024]{3,2,1,0:T(8,128)(2,1)}, bf16[8,4,32,1024]{3,2,1,0:T(8,128)(2,1)}, f32[8,16,8,256]{3,2,1,0:T(8,128)}) custom-call(f32[16,8,1024]{2,1,0:T(8,128)} %bitcast.11, bf16[4,32,1024]{2,1,0:T(8,128)(2,1)} %bitcast.13), custom_call_target="tpu_custom_call" | custom-call | tf_op jit(solution)/shard_map/exchange_panel/pallas_call | solution.py:612
  263.7 0.0 copy-start.1
  263.7 1.6 copy-done.1
  265.3 0.0 copy-start.2
  265.3 1.2 copy-done.2
  266.5 14.3 %update.1 = f32[1024,2048]{1,0:T(8,128)} custom-call(f32[1024,2048]{1,0:T(8,128)} %assemble.1.s_ref, bf16[1024,1024]{1,0:T(8,128)(2,1)S(1)} %bitcast.9, bf16[2048,1024]{1,0:T(8,128)(2,1)} %bitcast.15, f32[1024,256]{1,0:T(8,128)S(1)} %bitcast.10), custom_call_target="tpu_custom_call" | custom-call | tf_op jit(solution)/shard_map/update/pallas_call | solution.py:663
Async XLA Ops:
  151.3 1.7 copy-start
  153.1 1.0 copy-start.4
  213.0 0.8 copy-start.3
  213.8 0.7 copy-start.5
  263.7 1.6 copy-start.1
  265.3 1.2 copy-start.2

commit v2 on v1

v2 whole, which is shorter than its diff:
```python
import jax
import jax.numpy as jnp
from jax import lax
from jax.experimental import pallas as pl
from jax.experimental.pallas import tpu as pltpu
from jax.sharding import PartitionSpec as P

N = 16384
TB = 256
KT = 8
PW = 1024
SCEN = 64
NB = 128
F32 = jnp.float32
BF16 = jnp.bfloat16
HIGHEST = lax.Precision.HIGHEST
MESH = pl.DeviceIdType.MESH
DMA = pltpu.SemaphoreType.DMA
NT = (((1,), (1,)), ((), ()))
TN = (((0,), (0,)), ((), ()))
MIB = 1024 * 1024

COMBOS = [
    (0, 0), (1, 0), (3, 0), (0, 1), (0, 3), (2, 0), (0, 2), (1, 1),
    (1, 3), (3, 1), (3, 3), (2, 1), (2, 3), (1, 2), (3, 2), (2, 2),
]


def plane_slots():
    slots = {}
    for e1, e2 in COMBOS:
        if e2 == 0:
            kinds = {0: (0, 1, 2, 3), 1: (0, 2, 3)}.get(e1, (2, 3))
        else:
            kinds = (2,) if e2 == 1 else ()
        for kind in kinds:
            slots[(e1, e2, kind)] = len(slots)
    return slots


SLOTS = plane_slots()


def rem4(v):
    return lax.rem(v + 8, 4)


def place():
    p = lax.axis_index("scen")
    q = lax.axis_index("col")
    return p, q, p // 4, lax.rem(p, 4), q // 2, lax.rem(q, 2)


def dev(x, y, z, c):
    return (x * 4 + y, z * 2 + c)


def remote(src, dst, send, recv, device):
    return pltpu.make_async_remote_copy(
        src_ref=src, dst_ref=dst, send_sem=send, recv_sem=recv,
        device_id=device, device_id_type=MESH,
    )


def greet(devices):
    bar = pltpu.get_barrier_semaphore()
    for d in devices:
        pl.semaphore_signal(bar, inc=1, device_id=d, device_id_type=MESH)
    pl.semaphore_wait(bar, len(devices))


def lane(v):
    return pl.multiple_of(v, 128)


class Plane:
    def __init__(self, own, tiles, send_sem, recv_sem):
        self.own, self.tiles = own, tiles
        self.send_sem, self.recv_sem = send_sem, recv_sem
        self.p, self.q, self.x, self.y, self.z, self.c = place()

    def geom(self, j):
        return 1 - j, j, 1 - 2 * j

    def tile(self, e1, e2, j):
        sx, sy, _ = self.geom(j)
        ox = rem4(self.x - e1 * sx + e2 * sy)
        oy = rem4(self.y - e1 * sy + e2 * sx)
        return 2 * (ox * 4 + oy) + j

    def event(self, e1, e2, extra=None):
        def body(j, _):
            sx, sy, d = self.geom(j)
            s = self.tile(e1, e2, j)
            dst = self.tiles(s)
            if (e1, e2) == (0, 0):
                src = self.own(j)
            else:
                src = dst
                remote(
                    src, src, self.send_sem.at[0],
                    self.recv_sem.at[(e1 * 4 + e2) * 2 + j], (self.p, self.q),
                ).wait_recv()

            def send(kind, first, sign, r1, r2):
                dx = sx * sign if first else -sy * sign
                dy = sy * sign if first else -sx * sign
                remote(
                    src, dst, self.send_sem.at[SLOTS[(e1, e2, kind)] * 2 + j],
                    self.recv_sem.at[(r1 * 4 + r2) * 2 + j],
                    dev(rem4(self.x + dx), rem4(self.y + dy), self.z, self.c),
                ).start()

            if e2 == 0:
                if e1 == 0:
                    send(0, True, 1, 1, 0)
                    send(1, True, -1, 3, 0)
                if e1 == 1:
                    send(0, True, 1, 2, 0)
                send(2, False, 1, e1, 1)
                send(3, False, -1, e1, 3)
            elif e2 == 1:
                send(2, False, 1, e1, 2)
            if extra is not None:
                extra(src, s, (e1 * 4 + e2) * 2 + j, d)
            return 0

        lax.fori_loop(0, 2, body, 0)

    def drain(self):
        t = self.tiles(0)

        def body(i, _):
            remote(t, t, self.send_sem.at[i], self.recv_sem.at[0], (self.p, self.q)).wait_send()
            return 0

        lax.fori_loop(0, 2 * len(SLOTS), body, 0)


def plane_peers():
    p, q, x, y, z, c = place()
    return [
        dev(rem4(x + 1), y, z, c), dev(rem4(x - 1), y, z, c),
        dev(x, rem4(y + 1), z, c), dev(x, rem4(y - 1), z, c),
    ]


def relay_steps(plane, h_ref, zsem, psem, hsem):
    p, q, x, y, z, c = place()
    k = lax.rem(p, 8)
    zs, cs = k // 2, lax.rem(k, 2)
    here, partner = (p, q), dev(x, y, z, 1 - c)
    chain = c == cs
    source = jnp.logical_and(chain, z == zs)

    def feed(src, s, h, d):
        @pl.when(source)
        def _():
            remote(src, h_ref.at[s], zsem.at[h], hsem.at[h], dev(x, y, rem4(z + d), c)).start()
            remote(src, h_ref.at[s], psem.at[h], hsem.at[h], partner).start()

    def relay(e1, e2, r):
        def body(j, _):
            d = 1 - 2 * j
            h = (e1 * 4 + e2) * 2 + j

            @pl.when(jnp.logical_and(chain, rem4((z - zs) * d) == r))
            def _():
                t = h_ref.at[plane.tile(e1, e2, j)]
                remote(t, t, zsem.at[0], hsem.at[h], here).wait_recv()
                if r < 3:
                    remote(t, t, zsem.at[h], hsem.at[h], dev(x, y, rem4(z + d), c)).start()
                remote(t, t, psem.at[h], hsem.at[h], partner).start()

            return 0

        lax.fori_loop(0, 2, body, 0)

    def step(n):
        if n < len(COMBOS):
            plane.event(*COMBOS[n], extra=feed)
        for r in (1, 2, 3):
            if 0 <= n - r < len(COMBOS):
                relay(*COMBOS[n - r], r)

    def drain():
        t = h_ref.at[0]

        def last(i, _):
            d = 1 - 2 * lax.rem(i, 2)

            @pl.when(jnp.logical_and(chain, rem4((z - zs) * d) < 3))
            def _():
                remote(t, t, zsem.at[i], hsem.at[0], here).wait_send()

            @pl.when(chain)
            def _():
                remote(t, t, psem.at[i], hsem.at[0], here).wait_send()

            @pl.when(jnp.logical_not(chain))
            def _():
                remote(t, t, zsem.at[0], hsem.at[i], here).wait_recv()

            return 0

        lax.fori_loop(0, SCEN // 2, last, 0)

    return [lambda n=n: step(n) for n in range(len(COMBOS) + 3)], drain


PARTS = {
    (0, 0): [(0, 2)], (1, 0): [(0, 3), (1, 3)], (1, 1): [(1, 2)],
    (2, 0): [(0, 0), (2, 0)], (2, 1): [(0, 1), (3, 0)], (2, 2): [(2, 2)],
    (3, 0): [(1, 0), (2, 1)], (3, 1): [(1, 1), (3, 1)], (3, 2): [(2, 3), (3, 3)],
    (3, 3): [(3, 2)],
}


PACE = (1, 1, 1, 1, 1, 1, 1, 1)


def front_kernel(b_ref, bm_ref, bar_ref, g_ref, h_ref, w_ref,
                 xb, xc, part, rbuf, fin, zb, pk, v_ref,
                 loc, s1, r1, s2, r2, s3, r3, s4, r4, s5, r5,
                 ssem, rsem, zsem, psem, hsem):
    p, q, x, y, z, c = place()
    here, partner = (p, q), dev(x, y, z, 1 - c)
    greet([(lax.rem(p + i, 16), q) for i in range(1, 16)]
          + [(p, lax.rem(q + i, 8)) for i in range(1, 8)])
    own = pltpu.make_async_copy(b_ref, g_ref.at[pl.ds(2 * p, 2)], loc)
    own.start()
    plane = Plane(lambda j: b_ref.at[j], lambda s: g_ref.at[s], ssem, rsem)
    steps, drain = relay_steps(plane, h_ref, zsem, psem, hsem)

    def go(spot):
        for _ in range(min(len(steps), PACE[spot])):
            steps.pop(0)()

    go(0)
    holds = q < 4
    facing = dev(x, y, lax.rem(z + 1, 2), c)

    def to_partner():
        return remote(bm_ref, xb, s1.at[0], r1.at[0], partner)

    def to_facing():
        return remote(bm_ref.at[pl.ds(2 * lax.rem(z, 2), 2)], xc, s1.at[1], r1.at[1], facing)

    def slab(v):
        return v.reshape(v.shape[0] * TB, TB)

    def product(left, right):
        return lax.dot_general(slab(left), slab(right), TN, preferred_element_type=F32)

    def put(t, tile):
        part[:, t] = tile.reshape(16, 16, TB)

    def slices(i):
        g = lax.rem(p + i, 16)
        return remote(part.at[g], rbuf.at[p], s2.at[i - 1], r2.at[i - 1], (g, q))

    def halves(i):
        to = lax.rem(q + i, 8)
        return remote(fin.at[lax.rem(to, 2)], zb.at[q], s3.at[i - 1], r3.at[q], (p, to))

    @pl.when(holds)
    def _():
        to_facing().start()
        to_partner().start()
        put(2, product(bm_ref[...], bm_ref[...]))
        to_partner().wait_recv()

        def both(first, second):
            sl = pl.ds(2 * c, 2)
            put(3, product(second[sl], first[sl]))
            to_facing().wait_recv()

            @pl.when(z == 0)
            def _():
                put(0, product(xc[...], first[2:4]))
                put(1, product(xc[...], second[2:4]))

            @pl.when(z == 1)
            def _():
                put(0, product(first[0:2], xc[...]))
                put(1, product(second[0:2], xc[...]))

        @pl.when(c == 0)
        def _():
            both(bm_ref, xb)

        @pl.when(c == 1)
        def _():
            both(xb, bm_ref)

        for i in range(1, 16):
            slices(i).start()
        rbuf[p] = part[p]

    go(1)

    @pl.when(holds)
    def _():
        for i in range(1, 16):
            t = rbuf.at[lax.rem(p + 16 - i, 16)]
            remote(t, t, s2.at[i - 1], r2.at[i - 1], here).wait_recv()
        total = rbuf[0]
        for i in range(1, 16):
            total = total + rbuf[i]
        fin[0] = total[:, 0:8]
        fin[1] = total[:, 8:16]
        for i in range(1, 8):
            halves(i).start()
        zb[lax.rem(q, 4)] = fin[c]

    go(2)
    for m in range(4):
        @pl.when(q != m)
        def _():
            remote(zb.at[m], zb.at[m], s3.at[0], r3.at[m], here).wait_recv()

    at = (lax.broadcasted_iota(jnp.int32, (8, TB), 1)
          == p * 16 + c * 8 + lax.broadcasted_iota(jnp.int32, (8, TB), 0))
    for (k, m), parts in PARTS.items():
        v = zb[parts[0][0], parts[0][1]]
        for owner, t in parts[1:]:
            v = v + zb[owner, t]
        if k == m:
            v = v + jnp.where(at, bar_ref[k:k + 1, :], 0.0)
        first = (k * (k + 1) // 2 + m) * TB
        pk[p, c, :, first:first + TB] = v

    def shard(i):
        return remote(pk.at[p, c], pk.at[p, c], s4.at[i - 1], r4.at[i - 1],
                      (lax.rem(p + i, 16), q))

    def pass_on(i):
        t = pk.at[lax.rem(p + 16 - i, 16), c]
        return remote(t, t, s5.at[i], r5.at[i], partner)

    for i in range(1, 16):
        shard(i).start()
    pass_on(0).start()
    go(3)
    for i in range(1, 16):
        t = pk.at[lax.rem(p + 16 - i, 16), c]
        remote(t, t, s4.at[i - 1], r4.at[i - 1], here).wait_recv()
        pass_on(i).start()
        if i % 5 == 0:
            go(3 + i // 5)
    for i in range(16):
        t = pk.at[lax.rem(p + 16 - i, 16), 1 - c]
        remote(t, t, s5.at[i], r5.at[i], here).wait_recv()

    for k in range(4):
        width = TB * (k + 1)
        first = TB * (k * (k + 1) // 2)
        w_ref[TB * k:TB * (k + 1), 0:width] = pk[:, :, :, first:first + width].reshape(TB, width)
    blocks = PW // NB

    for n in range(blocks):
        lo, hi = NB * n, NB * (n + 1)
        turned = invert_factor(w_ref[lo:hi, lo:hi]).T
        go(7)
        v = jnp.dot(left_parts(w_ref[:, lo:hi]), right_parts(turned, 0),
                    preferred_element_type=F32)
        w_ref[:, lo:hi] = v
        w_ref[lo:hi, lo:hi] = turned
        if hi < PW:
            v_ref[...] = left_parts(w_ref[:, lo:hi])
            below = right_parts(w_ref[hi:PW, lo:hi], 1)
            w_ref[lo:hi, hi:PW] = jnp.zeros((NB, PW - hi), F32)
            for jl in range(hi, PW, TB):
                jh = min(jl + TB, PW)
                w_ref[:, jl:jh] -= lax.dot_general(
                    v_ref[...], below[jl - hi:jh - hi], NT, preferred_element_type=F32)
        go(7)
    while steps:
        steps.pop(0)()

    own.wait()
    plane.drain()
    drain()

    @pl.when(holds)
    def _():
        to_partner().wait_send()
        to_facing().wait_send()
        for i in range(1, 16):
            slices(i).wait_send()
        for i in range(1, 8):
            halves(i).wait_send()

    for i in range(1, 16):
        shard(i).wait_send()
    for i in range(16):
        pass_on(i).wait_send()


def front(border, masked, barrier):
    tiles = jax.ShapeDtypeStruct((SCEN // 2, 2, TB, TB), BF16)
    hbm = pl.BlockSpec(memory_space=pl.ANY)
    vmem = pl.BlockSpec(memory_space=pltpu.VMEM)
    return pl.pallas_call(
        front_kernel,
        out_shape=(tiles, tiles, jax.ShapeDtypeStruct((PW, PW), F32)),
        in_specs=[hbm, vmem, vmem],
        out_specs=(hbm, hbm, vmem),
        scratch_shapes=[
            pltpu.VMEM((4, TB, TB), BF16), pltpu.VMEM((2, TB, TB), BF16),
            pltpu.VMEM((16, 4, 16, TB), F32), pltpu.VMEM((16, 4, 16, TB), F32),
            pltpu.VMEM((2, 4, 8, TB), F32), pltpu.VMEM((4, 4, 8, TB), F32),
            pltpu.VMEM((16, 2, 8, 2560), F32), pltpu.VMEM((PW, 6 * NB), BF16),
            DMA(()), DMA((2,)), DMA((2,)), DMA((15,)), DMA((15,)), DMA((7,)), DMA((4,)),
            DMA((15,)), DMA((15,)), DMA((16,)), DMA((16,)),
            DMA((30,)), DMA((32,)), DMA((32,)), DMA((32,)), DMA((32,)),
        ],
        compiler_params=pltpu.CompilerParams(
            collective_id=0, has_side_effects=True, vmem_limit_bytes=48 * MIB),
        name="front",
    )(border.reshape(2, 2, TB, TB), masked, barrier)


PER_STEP = 4


def schur_kernel(touched_ref, g_ref, h_ref, bar_ref, out_ref):
    p, q = lax.axis_index("scen"), lax.axis_index("col")
    k = lax.rem(p, 8)
    step = pl.program_id(0)
    diagonal = k == q

    @pl.when(step == 0)
    def _():
        out_ref[...] = jnp.zeros_like(out_ref)

        @pl.when(diagonal)
        def _():
            eye = lax.broadcasted_iota(jnp.int32, (TB, TB), 0) == lax.broadcasted_iota(
                jnp.int32, (TB, TB), 1
            )
            for a in range(4):
                col = lane((2 * a + p // 8) * TB)
                row = bar_ref[pl.ds(a * 16 + p, 1), :]
                out_ref[a * TB:(a + 1) * TB, pl.ds(col, TB)] = jnp.where(eye, row, 0.0)

    for i in range(PER_STEP):
        s = step * PER_STEP + i
        big_row = touched_ref[s * KT + k]

        @pl.when(lax.rem(big_row, 16) == p)
        def _():
            row = pl.multiple_of((big_row // 16) * TB, TB)
            col = lane((touched_ref[s * KT + q] // 8) * TB)
            left = jnp.where(diagonal, g_ref[i], h_ref[i])
            out_ref[pl.ds(row, TB), pl.ds(col, TB)] += lax.dot_general(
                left, g_ref[i], TN, preferred_element_type=F32
            )


def assemble(touched, gathered, rows, barrier):
    block = pl.BlockSpec((PER_STEP, TB, TB), lambda i, t: (i, 0, 0))
    return pl.pallas_call(
        schur_kernel,
        out_shape=jax.ShapeDtypeStruct((1024, 2048), F32),
        grid_spec=pltpu.PrefetchScalarGridSpec(
            num_scalar_prefetch=1,
            grid=(SCEN // PER_STEP,),
            in_specs=[block, block, pl.BlockSpec((N // TB, TB), lambda i, t: (0, 0))],
            out_specs=pl.BlockSpec((1024, 2048), lambda i, t: (0, 0)),
        ),
        compiler_params=pltpu.CompilerParams(vmem_limit_bytes=48 * MIB),
        name="assemble",
    )(touched.reshape(-1), gathered.reshape(SCEN, TB, TB), rows.reshape(SCEN, TB, TB),
      barrier.reshape(N // TB, TB))


def pivot_pair(a, b, d):
    q0 = lax.rsqrt(a)
    q1 = lax.rsqrt(a * (a * d - b * b))
    inv = q1 * q1 * a
    return q0, q1, d * inv, b * inv, a * inv


def pivot_four(w):
    (w00,), (w10, w11), (w20, w21, w22), (w30, w31, w32, w33) = w
    q0, q1, ci, bi, ai = pivot_pair(w00, w10, w11)
    e02, e12 = ci * w20 - bi * w21, ai * w21 - bi * w20
    e03, e13 = ci * w30 - bi * w31, ai * w31 - bi * w30
    v22 = w22 - w20 * e02 - w21 * e12
    v32 = w32 - w30 * e02 - w31 * e12
    v33 = w33 - w30 * e03 - w31 * e13
    q2, q3, cj, bj, aj = pivot_pair(v22, v32, v33)

    def solve(r0, r1, r2, r3):
        z0, z1 = ci * r0 - bi * r1, ai * r1 - bi * r0
        s2, s3 = r2 - w20 * z0 - w21 * z1, r3 - w30 * z0 - w31 * z1
        z2, z3 = cj * s2 - bj * s3, aj * s3 - bj * s2
        return z0 - e02 * z2 - e03 * z3, z1 - e12 * z2 - e13 * z3, z2, z3, s2, s3

    def half(r0, r1, s2, s3):
        return [r0 * q0, (w00 * r1 - w10 * r0) * q1, s2 * q2, (v22 * s3 - v32 * s2) * q3]

    return solve, half


def splat(row, at):
    return jnp.broadcast_to(row[:, at:at + 1], (1, NB))


HB = NB // 2


def small_inverse(a):
    eye = (
        lax.broadcasted_iota(jnp.int32, (HB, HB), 0)
        == lax.broadcasted_iota(jnp.int32, (HB, HB), 1)
    ).astype(F32)
    t = jnp.concatenate([a, eye], axis=1)
    top, rows, w = 0, [], None
    for o in range(0, HB, 4):
        if 8 * (o // 8) > top:
            t, top = t[8 * (o // 8) - top:], 8 * (o // 8)
        k, height = o - top, t.shape[0]
        c = [jnp.broadcast_to(t[:, o + i:o + i + 1], (height, NB)) for i in range(4)]
        r = [t[k + i:k + i + 1, :] for i in range(4)]
        if w is None:
            w = [[c[v][k + u:k + u + 1, :] for v in range(u + 1)] for u in range(4)]
        solve, half = pivot_four(w)
        last = o + 4 == HB
        if not last:
            after = [t[k + 4 + i:k + 5 + i, :] for i in range(4)]
            g = [[splat(r[i], o + 4 + u) for u in range(4)] for i in range(4)]
            z = [solve(*[g[i][v] for i in range(4)]) for v in range(4)]
            w = [[splat(after[u], o + 4 + v)
                  - (g[0][u] * z[v][0] + g[1][u] * z[v][1])
                  - (g[2][u] * z[v][2] + g[3][u] * z[v][3]) for v in range(u + 1)]
                 for u in range(4)]
        z0, z1, z2, z3, s2, s3 = solve(*r)
        rows += half(r[0], r[1], s2, s3)
        if not last:
            t = t - (c[0] * z0 + c[1] * z1) - (c[2] * z2 + c[3] * z3)
    return jnp.concatenate(rows, 0)[:, HB:NB]


def wide(a, b, dims=(((1,), (0,)), ((), ()))):
    return lax.dot_general(a, b, dims, precision=HIGHEST, preferred_element_type=F32)


def thirds(v):
    a = v.astype(BF16)
    rest = v - a.astype(F32)
    b = rest.astype(BF16)
    return a, b, (rest - b.astype(F32)).astype(BF16)


def left_parts(v):
    a, b, c = thirds(v)
    return jnp.concatenate([a, a, b, b, a, c], axis=1)


def right_parts(v, axis):
    a, b, c = thirds(v)
    return jnp.concatenate([a, b, a, b, c, a], axis=axis)


def invert_factor(a):
    x1 = small_inverse(a[:HB, :HB])
    l = wide(a[HB:, :HB], x1, NT)
    x2 = small_inverse(a[HB:, HB:] - wide(l, l, NT))
    x21 = -wide(wide(x2, l), x1)
    return jnp.concatenate([
        jnp.concatenate([x1, jnp.zeros((HB, HB), F32)], 1),
        jnp.concatenate([x21, x2], 1)], 0)


def panel_kernel(s_ref, w_hbm, pc_ref, pr_ref, pan_ref, w_ref, raw_ref, pf_ref, pb_ref,
                 loc, asend, arecv, wsend, wrecv, ssem, rsem,
                 zsend, zrecv, csend, crecv, fsend, frecv):
    p, q, x, y, z, c = place()
    here, partner = (p, q), dev(x, y, z, 1 - c)
    twin = (8 * (p // 8) + q, lax.rem(p, 8))
    alone = lax.rem(p, 8) == q
    bar = pltpu.get_barrier_semaphore()
    for d in plane_peers() + [(p, lax.rem(q + i, 8)) for i in range(1, 8)]:
        pl.semaphore_signal(bar, inc=1, device_id=d, device_id_type=MESH)

    @pl.when(alone)
    def _():
        pl.semaphore_wait(bar, 11)

    @pl.when(jnp.logical_not(alone))
    def _():
        pl.semaphore_signal(bar, inc=1, device_id=twin, device_id_type=MESH)
        pl.semaphore_wait(bar, 12)

    holds = q < 4
    mine = lane(lax.rem(q, 4) * TB)

    def rows_to(i):
        to = lax.rem(q + i, 8)
        return remote(s_ref.at[pl.ds(16 * to, 16), :, pl.ds(0, TB)],
                      raw_ref.at[:, :, pl.ds(mine, TB)],
                      asend.at[i - 1], arecv.at[lax.rem(q, 4)], (p, to))

    own_rows = pltpu.make_async_copy(
        s_ref.at[pl.ds(16 * q, 16), :, pl.ds(0, TB)], raw_ref.at[:, :, pl.ds(mine, TB)], loc.at[0])
    inverse = pltpu.make_async_copy(w_hbm, w_ref, loc.at[1])

    @pl.when(holds)
    def _():
        for i in (2, 3, 4, 5, 6, 1, 7):
            rows_to(i).start()
        own_rows.start()

    inverse.start()
    for m in range(4):
        @pl.when(q == m)
        def _():
            own_rows.wait()

        @pl.when(q != m)
        def _():
            t = raw_ref.at[:, :, pl.ds(m * TB, TB)]
            remote(t, t, asend.at[0], arecv.at[m], here).wait_recv()

    inverse.wait()
    for n in range(PW // NB):
        lo, hi = NB * n, NB * (n + 1)
        v = jnp.dot(raw_ref[:, :, 0:hi].reshape(NB, hi), w_ref[0:hi, lo:hi],
                    precision=HIGHEST, preferred_element_type=F32)
        pf_ref[:, :, lo:hi] = v.reshape(16, 8, NB)
        pb_ref[:, :, lo:hi] = v.astype(BF16).reshape(2, 64, NB)

    def to_twin():
        return remote(pb_ref, pc_ref.at[twin[0]], wsend, wrecv, twin)

    keep_cols = pltpu.make_async_copy(pb_ref, pc_ref.at[p], loc.at[2])
    keep_rows = pltpu.make_async_copy(pb_ref, pr_ref.at[q], loc.at[3])

    @pl.when(alone)
    def _():
        keep_cols.start()

    @pl.when(jnp.logical_not(alone))
    def _():
        to_twin().start()

    keep_rows.start()

    def over(i):
        return remote(pb_ref, pr_ref.at[q], zsend.at[i - 1], zrecv.at[i - 1],
                      dev(x, y, rem4(z + i), c))

    def across(i):
        src = pb_ref if i == 0 else pr_ref.at[2 * rem4(z - i) + c]
        return remote(src, pr_ref.at[2 * rem4(z - i) + c], csend.at[i], crecv.at[i], partner)

    def block(m):
        return remote(pf_ref.at[:, :, pl.ds(m * TB, TB)], pan_ref.at[q],
                      fsend.at[m], frecv.at[q], (p, m))

    def block_here(m):
        return pltpu.make_async_copy(
            pf_ref.at[:, :, pl.ds(m * TB, TB)], pan_ref.at[q], loc.at[4])

    plane = Plane(lambda j: pc_ref.at[p, j], lambda s: pc_ref.at[s // 2, lax.rem(s, 2)], ssem, rsem)

    @pl.when(alone)
    def _():
        keep_cols.wait()

    @pl.when(jnp.logical_not(alone))
    def _():
        remote(pb_ref, pc_ref.at[p], wsend, wrecv, twin).wait_recv()

    for n in range(len(COMBOS)):
        plane.event(*COMBOS[n])
        if n == 0:
            for i in (1, 3, 2):
                over(i).start()
            across(0).start()
            for m in range(4):
                @pl.when(q != m)
                def _():
                    block(m).start()

                @pl.when(q == m)
                def _():
                    block_here(m).start()
        if n in (4, 6, 8):
            i = {4: 1, 6: 3, 8: 2}[n]
            t = pr_ref.at[2 * rem4(z - i) + c]
            remote(t, t, zsend.at[0], zrecv.at[i - 1], here).wait_recv()
            across(i).start()
    plane.drain()
    keep_rows.wait()
    for i in (1, 2, 3):
        over(i).wait_send()
    for i in range(4):
        across(i).wait_send()
        t = pr_ref.at[2 * rem4(z - i) + 1 - c]
        remote(t, t, csend.at[0], crecv.at[i], here).wait_recv()
    for m in range(4):
        @pl.when(q != m)
        def _():
            block(m).wait_send()

        @pl.when(q == m)
        def _():
            block_here(m).wait()
            for i in range(1, 8):
                t = pan_ref.at[lax.rem(q + i, 8)]
                remote(t, t, fsend.at[0], frecv.at[lax.rem(q + i, 8)], here).wait_recv()

    @pl.when(jnp.logical_not(alone))
    def _():
        to_twin().wait_send()

    @pl.when(holds)
    def _():
        for i in range(1, 8):
            rows_to(i).wait_send()


def solve_panel(schur, inverse):
    hbm = pl.BlockSpec(memory_space=pl.ANY)
    return pl.pallas_call(
        panel_kernel,
        out_shape=(
            jax.ShapeDtypeStruct((16, 2, 64, PW), BF16),
            jax.ShapeDtypeStruct((8, 2, 64, PW), BF16),
            jax.ShapeDtypeStruct((8, 16, 8, TB), F32),
        ),
        in_specs=[hbm, hbm],
        out_specs=(hbm, hbm, hbm),
        scratch_shapes=[
            pltpu.VMEM((PW, PW), F32), pltpu.VMEM((16, 8, PW), F32),
            pltpu.VMEM((16, 8, PW), F32), pltpu.VMEM((2, 64, PW), BF16),
            DMA((5,)), DMA((7,)), DMA((4,)), DMA(()), DMA(()), DMA((30,)), DMA((32,)),
            DMA((3,)), DMA((3,)), DMA((4,)), DMA((4,)), DMA((4,)), DMA((8,)),
        ],
        compiler_params=pltpu.CompilerParams(
            collective_id=1, has_side_effects=True, vmem_limit_bytes=32 * MIB),
        name="solve_panel",
    )(schur.reshape(128, 8, 2048), inverse)


STRIP = 128


def update_kernel(s_ref, pr_ref, pc_ref, pan_ref, out_ref):
    p, q = lax.axis_index("scen"), lax.axis_index("col")
    a = pl.program_id(0) // (TB // STRIP)
    low = jnp.logical_or(a > 0, p >= 4)
    panel = q < 4
    for b in range(8):
        cols = slice(b * TB, (b + 1) * TB)
        first = (b % 2) * 1024 + (b // 2) * TB

        def lowered():
            out_ref[:, cols] = s_ref[:, cols] - lax.dot_general(
                pr_ref[...], pc_ref[first:first + TB, :], NT, preferred_element_type=F32)

        def kept():
            out_ref[:, cols] = s_ref[:, cols]

        def solved():
            out_ref[:, cols] = pan_ref[...]

        if b == 0:
            pl.when(panel)(solved)
            pl.when(jnp.logical_and(jnp.logical_not(panel), low))(lowered)
            pl.when(jnp.logical_and(jnp.logical_not(panel), jnp.logical_not(low)))(kept)
        else:
            pl.when(low)(lowered)
            pl.when(jnp.logical_not(low))(kept)


def update(schur, rows, cols, panel):
    strip = pl.BlockSpec((STRIP, 2048), lambda i: (i, 0))
    return pl.pallas_call(
        update_kernel,
        out_shape=jax.ShapeDtypeStruct((1024, 2048), F32),
        grid=(1024 // STRIP,),
        in_specs=[
            strip,
            pl.BlockSpec((STRIP, PW), lambda i: (i, 0)),
            pl.BlockSpec((2048, PW), lambda i: (0, 0)),
            pl.BlockSpec((STRIP, TB), lambda i: (i, 0)),
        ],
        out_specs=strip,
        compiler_params=pltpu.CompilerParams(vmem_limit_bytes=48 * MIB),
        name="update",
    )(schur, rows.reshape(1024, PW), cols.reshape(2048, PW), panel.reshape(1024, TB))


def per_device(border, touched, barrier):
    p, q = lax.axis_index("scen"), lax.axis_index("col")
    mine = lax.dynamic_slice(touched, (4 * p, q), (4, 1))
    masked = jnp.where((mine == q)[:, :, None], border, jnp.zeros_like(border))
    gathered, rows, inverse = front(border, masked, barrier[:PW].reshape(4, TB))
    schur = assemble(touched, gathered, rows, barrier)
    panel_cols, panel_rows, panel = solve_panel(schur, inverse)
    return update(schur, panel_rows, panel_cols, panel)


def solution(mesh):
    in_specs = (P("scen", None, "col"), P(), P())
    out_specs = P("scen", "col")
    return jax.shard_map(
        per_device, mesh=mesh, in_specs=in_specs, out_specs=out_specs, check_vma=False
    )
```

time: 283 us -> 272 us (0.961)
  Pallas kernels: 272 us -> 258 us
    pallas_call x4 -> x2, Pallas kernels: 238 us -> 225 us  [the longest x1 137 us: front(): pl.pallas_call(front_kernel, out_shape=(tiles, tiles, jax.ShapeDtypeStruc...]
    unnamed x13 -> x7, local copies, waits for them, and re-layouts: 7.84 us -> 7.12 us
where the time goes in v2:
time: 272 us; the launch traced here: 269 us
  Pallas kernels  258 us (95%)
  local copies, waits for them, and re-layouts  8.77 us (3%)
    pallas_call x1, Pallas kernels, front(): pl.pallas_call(front_kernel, out_shape=(tiles, tiles, jax.ShapeDtypeStruc...  137 us
    pallas_call x1, Pallas kernels, solve_panel(): pl.pallas_call(panel_kernel, out_shape=(jax.ShapeDtypeStruct((16, 2, 64,...  88.5 us
    pallas_call x1, Pallas kernels, assemble(): pl.pallas_call(schur_kernel, out_shape=jax.ShapeDtypeStruct((1024, 2048),...  18.6 us
    pallas_call x1, Pallas kernels, update(): pl.pallas_call(update_kernel, out_shape=jax.ShapeDtypeStruct((1024, 2048)...  14.3 us
    unnamed x7, local copies, waits for them, and re-layouts  7.12 us

profile of v2, /device:TPU:0, one launch (start us, length us, event | category | flops | bytes accessed | tf_op | source)
XLA Modules:
  0.0 269.1 jit_solution(1864290321533379410)
XLA Ops:
  0.0 0.8 compare_bitcast_fusion
  0.8 0.7 slice.13
  1.5 0.8 copy.4
  2.2 0.1 reshape.37.touched_ref
  2.3 0.9 reshape.41.bar_ref
  3.2 1.2 broadcast_select_fusion.bm_ref
  4.3 0.0 copy-start.2
  4.4 1.0 copy-done.2
  5.4 136.7 %front.1 = (bf16[32,2,256,256]{3,2,1,0:T(8,128)(2,1)}, bf16[32,2,256,256]{3,2,1,0:T(8,128)(2,1)}, f32[1024,1024]{1,0:T(8,128)S(1)}) custom-call(bf16[2,2,256,256]{3,2,1,0:T(8,128)(2,1)S(1)} %bitcast.12, bf16[4,256,256]{2,1,0:T(8,128)(2,1)S(1)} %broadcast_select_fusion.bm_ref, f32[4,256]{1,0:T(4,128)S(1)} %slice.14.bar_ref), custom_call_target="tpu_custom_call" | custom-call | tf_op jit(solution)/shard_map/front/pallas_call | solution.py:404
  142.1 18.6 %assemble.1.s_ref = f32[1024,2048]{1,0:T(8,128)} custom-call(s32[512]{0:T(512)S(1)} %reshape.37.touched_ref, bf16[64,256,256]{2,1,0:T(8,128)(2,1)} %bitcast.14, bf16[64,256,256]{2,1,0:T(8,128)(2,1)} %bitcast.15, f32[64,256]{1,0:T(8,128)S(1)} %reshape.41.bar_ref), custom_call_target="tpu_custom_call" | custom-call | tf_op jit(solution)/shard_map/assemble/pallas_call | solution.py:463
  160.7 0.0 copy-start
  160.7 3.4 %copy-done = f32[1024,2048]{1,0:T(8,128)S(1)} copy-done((f32[1024,2048]{1,0:T(8,128)S(1)}, f32[1024,2048]{1,0:T(8,128)}, u32[]{:S(2)}) %copy-start) | copy-done | bytes 8388632
  164.1 88.5 %solve_panel.1 = (bf16[16,2,64,1024]{3,2,1,0:T(8,128)(2,1)S(1)}, bf16[8,2,64,1024]{3,2,1,0:T(8,128)(2,1)S(1)}, f32[8,16,8,256]{3,2,1,0:T(8,128)S(1)}) custom-call(f32[128,8,2048]{2,1,0:T(8,128)S(1)} %bitcast.9, f32[1024,1024]{1,0:T(8,128)S(1)} %get-tuple-element.13.w_hbm), custom_call_target="tpu_custom_call" | custom-call | tf_op jit(solution)/shard_map/solve_panel/pallas_call | solution.py:728
  252.6 0.0 copy-start.1
  252.6 1.9 copy-done.1
  254.5 14.3 %update.1 = f32[1024,2048]{1,0:T(8,128)} custom-call(f32[1024,2048]{1,0:T(8,128)} %assemble.1.s_ref, bf16[1024,1024]{1,0:T(8,128)(2,1)S(1)} %bitcast.11, bf16[2048,1024]{1,0:T(8,128)(2,1)} %bitcast.10, f32[1024,256]{1,0:T(8,128)S(1)} %bitcast.13), custom_call_target="tpu_custom_call" | custom-call | tf_op jit(solution)/shard_map/update/pallas_call | solution.py:782
  (1 shorter events, 0.0 us)
Async XLA Ops:
  4.3 1.0 copy-start.2
  160.7 3.4 %copy-start = (f32[1024,2048]{1,0:T(8,128)S(1)}, f32[1024,2048]{1,0:T(8,128)}, u32[]{:S(2)}) copy-start(f32[1024,2048]{1,0:T(8,128)} %assemble.1.s_ref) | copy-start | bytes 25165828
  252.6 1.9 copy-start.1

commit v3 on v2

--- a/solution.py
+++ b/solution.py
@@ -74,23 +74,28 @@
 
 
 class Plane:
-    def __init__(self, own, tiles, send_sem, recv_sem):
+    def __init__(self, count, own, tiles, send_sem, recv_sem):
+        self.count = count
         self.own, self.tiles = own, tiles
         self.send_sem, self.recv_sem = send_sem, recv_sem
         self.p, self.q, self.x, self.y, self.z, self.c = place()
 
     def geom(self, j):
-        return 1 - j, j, 1 - 2 * j
+        if self.count == 2:
+            return 1 - j, j, 1, -1
+        sy = j // 2
+        d = 1 - 2 * lax.rem(j, 2)
+        return 1 - sy, sy, d, d
 
     def tile(self, e1, e2, j):
-        sx, sy, _ = self.geom(j)
-        ox = rem4(self.x - e1 * sx + e2 * sy)
-        oy = rem4(self.y - e1 * sy + e2 * sx)
-        return 2 * (ox * 4 + oy) + j
+        sx, sy, d1, d2 = self.geom(j)
+        ox = rem4(self.x - d1 * e1 * sx - d2 * e2 * sy)
+        oy = rem4(self.y - d1 * e1 * sy - d2 * e2 * sx)
+        return self.count * (ox * 4 + oy) + j
 
     def event(self, e1, e2, extra=None):
         def body(j, _):
-            sx, sy, d = self.geom(j)
+            sx, sy, d1, d2 = self.geom(j)
             s = self.tile(e1, e2, j)
             dst = self.tiles(s)
             if (e1, e2) == (0, 0):
@@ -99,15 +104,15 @@
                 src = dst
                 remote(
                     src, src, self.send_sem.at[0],
-                    self.recv_sem.at[(e1 * 4 + e2) * 2 + j], (self.p, self.q),
+                    self.recv_sem.at[(e1 * 4 + e2) * self.count + j], (self.p, self.q),
                 ).wait_recv()
 
             def send(kind, first, sign, r1, r2):
-                dx = sx * sign if first else -sy * sign
-                dy = sy * sign if first else -sx * sign
+                dx = sx * d1 * sign if first else sy * d2 * sign
+                dy = sy * d1 * sign if first else sx * d2 * sign
                 remote(
-                    src, dst, self.send_sem.at[SLOTS[(e1, e2, kind)] * 2 + j],
-                    self.recv_sem.at[(r1 * 4 + r2) * 2 + j],
+                    src, dst, self.send_sem.at[SLOTS[(e1, e2, kind)] * self.count + j],
+                    self.recv_sem.at[(r1 * 4 + r2) * self.count + j],
                     dev(rem4(self.x + dx), rem4(self.y + dy), self.z, self.c),
                 ).start()
 
@@ -122,10 +127,10 @@
             elif e2 == 1:
                 send(2, False, 1, e1, 2)
             if extra is not None:
-                extra(src, s, (e1 * 4 + e2) * 2 + j, d)
+                extra(src, s, (e1 * 4 + e2) * 2 + j, 1 - 2 * j)
             return 0
 
-        lax.fori_loop(0, 2, body, 0)
+        lax.fori_loop(0, self.count, body, 0)
 
     def drain(self):
         t = self.tiles(0)
@@ -134,7 +139,7 @@
             remote(t, t, self.send_sem.at[i], self.recv_sem.at[0], (self.p, self.q)).wait_send()
             return 0
 
-        lax.fori_loop(0, 2 * len(SLOTS), body, 0)
+        lax.fori_loop(0, self.count * len(SLOTS), body, 0)
 
 
 def plane_peers():
@@ -180,8 +185,8 @@
         if n < len(COMBOS):
             plane.event(*COMBOS[n], extra=feed)
         for r in (1, 2, 3):
-            if 0 <= n - r < len(COMBOS):
-                relay(*COMBOS[n - r], r)
+            if 0 <= n - 2 * r < len(COMBOS):
+                relay(*COMBOS[n - 2 * r], r)
 
     def drain():
         t = h_ref.at[0]
@@ -205,7 +210,7 @@
 
         lax.fori_loop(0, SCEN // 2, last, 0)
 
-    return [lambda n=n: step(n) for n in range(len(COMBOS) + 3)], drain
+    return [lambda n=n: step(n) for n in range(len(COMBOS) + 6)], drain
 
 
 PARTS = {
@@ -229,7 +234,7 @@
           + [(p, lax.rem(q + i, 8)) for i in range(1, 8)])
     own = pltpu.make_async_copy(b_ref, g_ref.at[pl.ds(2 * p, 2)], loc)
     own.start()
-    plane = Plane(lambda j: b_ref.at[j], lambda s: g_ref.at[s], ssem, rsem)
+    plane = Plane(2, lambda j: b_ref.at[j], lambda s: g_ref.at[s], ssem, rsem)
     steps, drain = relay_steps(plane, h_ref, zsem, psem, hsem)
 
     def go(spot):
@@ -424,7 +429,9 @@
 PER_STEP = 4
 
 
-def schur_kernel(touched_ref, g_ref, h_ref, bar_ref, out_ref):
+def schur_kernel(touched_ref, list_ref, count_ref, *refs):
+    g_refs, h_refs = refs[:PER_STEP], refs[PER_STEP:2 * PER_STEP]
+    bar_ref, out_ref, prod_ref = refs[2 * PER_STEP:]
     p, q = lax.axis_index("scen"), lax.axis_index("col")
     k = lax.rem(p, 8)
     step = pl.program_id(0)
@@ -444,35 +451,48 @@
                 row = bar_ref[pl.ds(a * 16 + p, 1), :]
                 out_ref[a * TB:(a + 1) * TB, pl.ds(col, TB)] = jnp.where(eye, row, 0.0)
 
-    for i in range(PER_STEP):
-        s = step * PER_STEP + i
-        big_row = touched_ref[s * KT + k]
-
-        @pl.when(lax.rem(big_row, 16) == p)
-        def _():
-            row = pl.multiple_of((big_row // 16) * TB, TB)
-            col = lane((touched_ref[s * KT + q] // 8) * TB)
-            left = jnp.where(diagonal, g_ref[i], h_ref[i])
-            out_ref[pl.ds(row, TB), pl.ds(col, TB)] += lax.dot_general(
-                left, g_ref[i], TN, preferred_element_type=F32
-            )
+    @pl.when(step * PER_STEP < count_ref[0])
+    def _():
+        for i in range(PER_STEP):
+            right = g_refs[i][0]
+            left = jnp.where(diagonal, right, h_refs[i][0])
+            prod_ref[i] = lax.dot_general(left, right, TN, preferred_element_type=F32)
+
+        for i in range(PER_STEP):
+            @pl.when(step * PER_STEP + i < count_ref[0])
+            def _():
+                s = list_ref[step * PER_STEP + i]
+                row = pl.multiple_of((touched_ref[s, k] // 16) * TB, TB)
+                col = lane((touched_ref[s, q] // 8) * TB)
+                out_ref[pl.ds(row, TB), pl.ds(col, TB)] += prod_ref[i]
 
 
 def assemble(touched, gathered, rows, barrier):
-    block = pl.BlockSpec((PER_STEP, TB, TB), lambda i, t: (i, 0, 0))
+    p = lax.axis_index("scen")
+    index = jnp.arange(SCEN, dtype=jnp.int32)
+    mine = lax.dynamic_index_in_dim(touched, lax.rem(p, 8), 1, keepdims=False) % 16 == p
+    place_of = jnp.sum(jnp.where(mine[None, :] & (index[None, :] < index[:, None]), 1, 0), axis=1)
+    listed = jnp.sum(
+        jnp.where(mine[None, :] & (place_of[None, :] == index[:, None]), index[None, :], 0), axis=1)
+    count = jnp.sum(mine.astype(jnp.int32)).reshape(1)
+    blocks = [
+        pl.BlockSpec((1, TB, TB), lambda i, t, l, c, j=j: (l[i * PER_STEP + j], 0, 0))
+        for j in range(PER_STEP)
+    ]
     return pl.pallas_call(
         schur_kernel,
         out_shape=jax.ShapeDtypeStruct((1024, 2048), F32),
         grid_spec=pltpu.PrefetchScalarGridSpec(
-            num_scalar_prefetch=1,
+            num_scalar_prefetch=3,
             grid=(SCEN // PER_STEP,),
-            in_specs=[block, block, pl.BlockSpec((N // TB, TB), lambda i, t: (0, 0))],
-            out_specs=pl.BlockSpec((1024, 2048), lambda i, t: (0, 0)),
+            in_specs=blocks + blocks + [pl.BlockSpec((N // TB, TB), lambda i, t, l, c: (0, 0))],
+            out_specs=pl.BlockSpec((1024, 2048), lambda i, t, l, c: (0, 0)),
+            scratch_shapes=[pltpu.VMEM((PER_STEP, TB, TB), F32)],
         ),
-        compiler_params=pltpu.CompilerParams(vmem_limit_bytes=48 * MIB),
+        compiler_params=pltpu.CompilerParams(vmem_limit_bytes=60 * MIB),
         name="assemble",
-    )(touched.reshape(-1), gathered.reshape(SCEN, TB, TB), rows.reshape(SCEN, TB, TB),
-      barrier.reshape(N // TB, TB))
+    )(touched, listed, count, *[gathered.reshape(SCEN, TB, TB)] * PER_STEP,
+      *[rows.reshape(SCEN, TB, TB)] * PER_STEP, barrier)
 
 
 def pivot_pair(a, b, d):
@@ -630,7 +650,7 @@
         v = jnp.dot(raw_ref[:, :, 0:hi].reshape(NB, hi), w_ref[0:hi, lo:hi],
                     precision=HIGHEST, preferred_element_type=F32)
         pf_ref[:, :, lo:hi] = v.reshape(16, 8, NB)
-        pb_ref[:, :, lo:hi] = v.astype(BF16).reshape(2, 64, NB)
+        pb_ref[:, :, lo:hi] = v.astype(BF16).reshape(4, 32, NB)
 
     def to_twin():
         return remote(pb_ref, pc_ref.at[twin[0]], wsend, wrecv, twin)
@@ -664,7 +684,8 @@
         return pltpu.make_async_copy(
             pf_ref.at[:, :, pl.ds(m * TB, TB)], pan_ref.at[q], loc.at[4])
 
-    plane = Plane(lambda j: pc_ref.at[p, j], lambda s: pc_ref.at[s // 2, lax.rem(s, 2)], ssem, rsem)
+    plane = Plane(
+        4, lambda j: pc_ref.at[p, j], lambda s: pc_ref.at[s // 4, lax.rem(s, 4)], ssem, rsem)
 
     @pl.when(alone)
     def _():
@@ -728,16 +749,16 @@
     return pl.pallas_call(
         panel_kernel,
         out_shape=(
-            jax.ShapeDtypeStruct((16, 2, 64, PW), BF16),
-            jax.ShapeDtypeStruct((8, 2, 64, PW), BF16),
+            jax.ShapeDtypeStruct((16, 4, 32, PW), BF16),
+            jax.ShapeDtypeStruct((8, 4, 32, PW), BF16),
             jax.ShapeDtypeStruct((8, 16, 8, TB), F32),
         ),
         in_specs=[hbm, hbm],
         out_specs=(hbm, hbm, hbm),
         scratch_shapes=[
             pltpu.VMEM((PW, PW), F32), pltpu.VMEM((16, 8, PW), F32),
-            pltpu.VMEM((16, 8, PW), F32), pltpu.VMEM((2, 64, PW), BF16),
-            DMA((5,)), DMA((7,)), DMA((4,)), DMA(()), DMA(()), DMA((30,)), DMA((32,)),
+            pltpu.VMEM((16, 8, PW), F32), pltpu.VMEM((4, 32, PW), BF16),
+            DMA((5,)), DMA((7,)), DMA((4,)), DMA(()), DMA(()), DMA((60,)), DMA((64,)),
             DMA((3,)), DMA((3,)), DMA((4,)), DMA((4,)), DMA((4,)), DMA((8,)),
         ],
         compiler_params=pltpu.CompilerParams(
@@ -746,7 +767,7 @@
     )(schur.reshape(128, 8, 2048), inverse)
 
 
-STRIP = 128
+STRIP = 256
 
 
 def update_kernel(s_ref, pr_ref, pc_ref, pan_ref, out_ref):
@@ -799,7 +820,8 @@
     p, q = lax.axis_index("scen"), lax.axis_index("col")
     mine = lax.dynamic_slice(touched, (4 * p, q), (4, 1))
     masked = jnp.where((mine == q)[:, :, None], border, jnp.zeros_like(border))
-    gathered, rows, inverse = front(border, masked, barrier[:PW].reshape(4, TB))
+    barrier = barrier.reshape(N // TB, TB)
+    gathered, rows, inverse = front(border, masked, barrier)
     schur = assemble(touched, gathered, rows, barrier)
     panel_cols, panel_rows, panel = solve_panel(schur, inverse)
     return update(schur, panel_rows, panel_cols, panel)

time: 272 us -> 234 us (0.86)
  Pallas kernels: 258 us -> 213 us
  local copies, waits for them, and re-layouts: 8.77 us -> 12.8 us
    pallas_call x1, Pallas kernels: 88.5 us -> 64.9 us  [solve_panel(): pl.pallas_call(panel_kernel, out_shape=(jax.ShapeDtypeStruct((16, 4, 32,...]
    pallas_call x1, Pallas kernels: 137 us -> 125 us  [front(): pl.pallas_call(front_kernel, out_shape=(tiles, tiles, jax.ShapeDtypeStruc...]
    pallas_call x1, Pallas kernels: 18.6 us -> 13.5 us  [assemble(): pl.pallas_call(schur_kernel, out_shape=jax.ShapeDtypeStruct((1024, 2048),...]
    unnamed x7 -> x13, local copies, waits for them, and re-layouts: 7.12 us -> 12 us
    pallas_call x1, Pallas kernels: 14.3 us -> 9.63 us  [update(): pl.pallas_call(update_kernel, out_shape=jax.ShapeDtypeStruct((1024, 2048)...]
where the time goes in v3:
time: 234 us; the launch traced here: 231 us
  Pallas kernels  213 us (91%)
  local copies, waits for them, and re-layouts  12.8 us (5%)
  other arithmetic  4.13 us (2%)
    pallas_call x1, Pallas kernels, front(): pl.pallas_call(front_kernel, out_shape=(tiles, tiles, jax.ShapeDtypeStruc...  125 us
    pallas_call x1, Pallas kernels, solve_panel(): pl.pallas_call(panel_kernel, out_shape=(jax.ShapeDtypeStruct((16, 4, 32,...  64.9 us
    pallas_call x1, Pallas kernels, assemble(): pl.pallas_call(schur_kernel, out_shape=jax.ShapeDtypeStruct((1024, 2048),...  13.5 us
    unnamed x13, local copies, waits for them, and re-layouts  12 us
    pallas_call x1, Pallas kernels, update(): pl.pallas_call(update_kernel, out_shape=jax.ShapeDtypeStruct((1024, 2048)...  9.63 us

profile of v3, /device:TPU:0, one launch (start us, length us, event | category | flops | bytes accessed | tf_op | source)
XLA Modules:
  0.0 230.6 jit_solution(13146050380316048170)
XLA Ops:
  0.0 0.8 compare_bitcast_fusion
  0.8 1.4 convert_reduce_fusion
  2.2 0.1 select_reduce_fusion.1
  2.3 0.7 select_reduce_fusion.list_ref
  3.0 1.4 copy.5.touched_ref
  4.3 0.9 reshape.53.bar_ref.refs_8_
  5.2 0.0 copy-start.5
  5.2 1.2 broadcast_select_fusion.bm_ref
  6.4 0.0 copy-start.4
  6.4 1.0 copy-done.4
  7.4 125.3 %front.1 = (bf16[32,2,256,256]{3,2,1,0:T(8,128)(2,1)}, bf16[32,2,256,256]{3,2,1,0:T(8,128)(2,1)}, f32[1024,1024]{1,0:T(8,128)S(1)}) custom-call(bf16[2,2,256,256]{3,2,1,0:T(8,128)(2,1)S(1)} %bitcast.16, bf16[4,256,256]{2,1,0:T(8,128)(2,1)S(1)} %broadcast_select_fusion.bm_ref, f32[64,256]{1,0:T(8,128)S(1)} %reshape.53.bar_ref.refs_8_), custom_call_target="tpu_custom_call" | custom-call | tf_op jit(solution)/shard_map/front/pallas_call | solution.py:409
  132.8 0.0 copy-start.1
  132.8 2.0 copy-done.1
  134.8 0.0 copy-done.5
  134.8 13.5 %assemble.1.s_ref = f32[1024,2048]{1,0:T(8,128)} custom-call(s32[64,8]{1,0:T(8,128)} %copy.5.touched_ref, s32[64]{0:T(128)} %select_reduce_fusion.list_ref, s32[1]{0:T(128)} %bitcast.1.count_ref, bf16[64,256,256]{2,1,0:T(8,128)(2,1)} %bitcast.18, bf16[64,256,256]{2,1,0:T(8,128)(2,1)} %bitcast.19, bf16[64,256,256]{2,1,0:T(8,128)(2,1)} %bitcast.20, ...), custom_call_target="tpu_custom_call" | custom-call | tf_op jit(solution)/shard_map/assemble/pallas_call | solution.py:482
  148.3 0.0 copy-start
  148.3 3.4 %copy-done = f32[1024,2048]{1,0:T(8,128)S(1)} copy-done((f32[1024,2048]{1,0:T(8,128)S(1)}, f32[1024,2048]{1,0:T(8,128)}, u32[]{:S(2)}) %copy-start) | copy-done | bytes 8388632
  151.7 0.0 copy-start.2
  151.7 2.2 copy-done.2
  153.9 64.9 %solve_panel.1 = (bf16[16,4,32,1024]{3,2,1,0:T(8,128)(2,1)S(1)}, bf16[8,4,32,1024]{3,2,1,0:T(8,128)(2,1)S(1)}, f32[8,16,8,256]{3,2,1,0:T(8,128)S(1)}) custom-call(f32[128,8,2048]{2,1,0:T(8,128)S(1)} %bitcast.13, f32[1024,1024]{1,0:T(8,128)S(1)} %copy-done.2), custom_call_target="tpu_custom_call" | custom-call | tf_op jit(solution)/shard_map/solve_panel/pallas_call | solution.py:749
  218.8 0.0 copy-start.3
  218.8 2.0 copy-done.3
  220.8 9.6 %update.1 = f32[1024,2048]{1,0:T(8,128)} custom-call(f32[1024,2048]{1,0:T(8,128)} %assemble.1.s_ref, bf16[1024,1024]{1,0:T(8,128)(2,1)S(1)} %bitcast.15, bf16[2048,1024]{1,0:T(8,128)(2,1)} %bitcast.14, f32[1024,256]{1,0:T(8,128)S(1)} %bitcast.17), custom_call_target="tpu_custom_call" | custom-call | tf_op jit(solution)/shard_map/update/pallas_call | solution.py:803
Async XLA Ops:
  5.2 129.6 %copy-start.5 = (f32[64,256]{1,0:T(8,128)}, f32[64,256]{1,0:T(8,128)S(1)}, u32[]{:S(2)}) copy-start(f32[64,256]{1,0:T(8,128)S(1)} %reshape.53.bar_ref.refs_8_) | copy-start | bytes 196612
  6.4 1.0 copy-start.4
  132.8 2.0 copy-start.1
  148.3 3.4 %copy-start = (f32[1024,2048]{1,0:T(8,128)S(1)}, f32[1024,2048]{1,0:T(8,128)}, u32[]{:S(2)}) copy-start(f32[1024,2048]{1,0:T(8,128)} %assemble.1.s_ref) | copy-start | bytes 25165828
  151.7 2.2 copy-start.2
  218.8 2.0 copy-start.3

commit v4 on v3

--- a/solution.py
+++ b/solution.py
@@ -224,9 +224,9 @@
 PACE = (1, 1, 1, 1, 1, 1, 1, 1)
 
 
-def front_kernel(b_ref, bm_ref, bar_ref, g_ref, h_ref, w_ref,
-                 xb, xc, part, rbuf, fin, zb, pk, v_ref,
-                 loc, s1, r1, s2, r2, s3, r3, s4, r4, s5, r5,
+def front_kernel(b_ref, bm_ref, bar_ref, g_ref, h_ref, w_out,
+                 xb, xc, part, rbuf, fin, zb, pk, v_ref, w_ref,
+                 loc, wloc, s1, r1, s2, r2, s3, r3, s4, r4, s5, r5,
                  ssem, rsem, zsem, psem, hsem):
     p, q, x, y, z, c = place()
     here, partner = (p, q), dev(x, y, z, 1 - c)
@@ -380,10 +380,13 @@
                 w_ref[:, jl:jh] -= lax.dot_general(
                     v_ref[...], below[jl - hi:jh - hi], NT, preferred_element_type=F32)
         go(7)
+    keep = pltpu.make_async_copy(w_ref, w_out, wloc)
+    keep.start()
     while steps:
         steps.pop(0)()
 
     own.wait()
+    keep.wait()
     plane.drain()
     drain()
 
@@ -410,18 +413,19 @@
         front_kernel,
         out_shape=(tiles, tiles, jax.ShapeDtypeStruct((PW, PW), F32)),
         in_specs=[hbm, vmem, vmem],
-        out_specs=(hbm, hbm, vmem),
+        out_specs=(hbm, hbm, hbm),
         scratch_shapes=[
             pltpu.VMEM((4, TB, TB), BF16), pltpu.VMEM((2, TB, TB), BF16),
             pltpu.VMEM((16, 4, 16, TB), F32), pltpu.VMEM((16, 4, 16, TB), F32),
             pltpu.VMEM((2, 4, 8, TB), F32), pltpu.VMEM((4, 4, 8, TB), F32),
             pltpu.VMEM((16, 2, 8, 2560), F32), pltpu.VMEM((PW, 6 * NB), BF16),
-            DMA(()), DMA((2,)), DMA((2,)), DMA((15,)), DMA((15,)), DMA((7,)), DMA((4,)),
+            pltpu.VMEM((PW, PW), F32),
+            DMA(()), DMA(()), DMA((2,)), DMA((2,)), DMA((15,)), DMA((15,)), DMA((7,)), DMA((4,)),
             DMA((15,)), DMA((15,)), DMA((16,)), DMA((16,)),
             DMA((30,)), DMA((32,)), DMA((32,)), DMA((32,)), DMA((32,)),
         ],
         compiler_params=pltpu.CompilerParams(
-            collective_id=0, has_side_effects=True, vmem_limit_bytes=48 * MIB),
+            collective_id=0, has_side_effects=True, vmem_limit_bytes=60 * MIB),
         name="front",
     )(border.reshape(2, 2, TB, TB), masked, barrier)
 
@@ -462,8 +466,8 @@
             @pl.when(step * PER_STEP + i < count_ref[0])
             def _():
                 s = list_ref[step * PER_STEP + i]
-                row = pl.multiple_of((touched_ref[s, k] // 16) * TB, TB)
-                col = lane((touched_ref[s, q] // 8) * TB)
+                row = pl.multiple_of((touched_ref[s * KT + k] // 16) * TB, TB)
+                col = lane((touched_ref[s * KT + q] // 8) * TB)
                 out_ref[pl.ds(row, TB), pl.ds(col, TB)] += prod_ref[i]
 
 
@@ -491,7 +495,7 @@
         ),
         compiler_params=pltpu.CompilerParams(vmem_limit_bytes=60 * MIB),
         name="assemble",
-    )(touched, listed, count, *[gathered.reshape(SCEN, TB, TB)] * PER_STEP,
+    )(touched.reshape(-1), listed, count, *[gathered.reshape(SCEN, TB, TB)] * PER_STEP,
       *[rows.reshape(SCEN, TB, TB)] * PER_STEP, barrier)
 
 
@@ -762,7 +766,7 @@
             DMA((3,)), DMA((3,)), DMA((4,)), DMA((4,)), DMA((4,)), DMA((8,)),
         ],
         compiler_params=pltpu.CompilerParams(
-            collective_id=1, has_side_effects=True, vmem_limit_bytes=32 * MIB),
+            collective_id=1, has_side_effects=True, vmem_limit_bytes=60 * MIB),
         name="solve_panel",
     )(schur.reshape(128, 8, 2048), inverse)
 
@@ -811,7 +815,7 @@
             pl.BlockSpec((STRIP, TB), lambda i: (i, 0)),
         ],
         out_specs=strip,
-        compiler_params=pltpu.CompilerParams(vmem_limit_bytes=48 * MIB),
+        compiler_params=pltpu.CompilerParams(vmem_limit_bytes=60 * MIB),
         name="update",
     )(schur, rows.reshape(1024, PW), cols.reshape(2048, PW), panel.reshape(1024, TB))
 

time: 234 us -> 231 us (0.987)
  local copies, waits for them, and re-layouts: 12.8 us -> 2.87 us
  Pallas kernels: 213 us -> 218 us
    unnamed x13 -> x1, local copies, waits for them, and re-layouts: 12 us -> 0.77 us
    pallas_call x1, Pallas kernels: 125 us -> 130 us  [front(): pl.pallas_call(front_kernel, out_shape=(tiles, tiles, jax.ShapeDtypeStruc...]
where the time goes in v4:
time: 231 us; the launch traced here: 227 us
  Pallas kernels  218 us (94%)
  other arithmetic  4.9 us (2%)
  local copies, waits for them, and re-layouts  2.87 us (1%)
    pallas_call x1, Pallas kernels, front(): pl.pallas_call(front_kernel, out_shape=(tiles, tiles, jax.ShapeDtypeStruc...  130 us
    pallas_call x1, Pallas kernels, solve_panel(): pl.pallas_call(panel_kernel, out_shape=(jax.ShapeDtypeStruct((16, 4, 32,...  62.8 us
    pallas_call x1, Pallas kernels, assemble(): pl.pallas_call(schur_kernel, out_shape=jax.ShapeDtypeStruct((1024, 2048),...  15.3 us
    pallas_call x1, Pallas kernels, update(): pl.pallas_call(update_kernel, out_shape=jax.ShapeDtypeStruct((1024, 2048)...  10.3 us

profile of v4, /device:TPU:0, one launch (start us, length us, event | category | flops | bytes accessed | tf_op | source)
XLA Modules:
  0.0 226.6 jit_solution(11438434210454850794)
XLA Ops:
  0.0 0.8 compare_bitcast_fusion
  0.8 1.4 convert_reduce_fusion
  2.2 0.1 select_reduce_fusion.1
  2.3 0.7 select_reduce_fusion.list_ref
  3.0 0.8 copy.5
  3.7 0.6 reshape.54.touched_ref
  4.4 1.5 reshape.57.bar_ref.refs_8_
  5.8 1.9 broadcast_select_fusion.bm_ref
  7.8 130.1 %front.1 = (bf16[32,2,256,256]{3,2,1,0:T(8,128)(2,1)}, bf16[32,2,256,256]{3,2,1,0:T(8,128)(2,1)}, f32[1024,1024]{1,0:T(8,128)}) custom-call(bf16[2,2,256,256]{3,2,1,0:T(8,128)(2,1)} %bitcast.24, bf16[4,256,256]{2,1,0:T(8,128)(2,1)} %broadcast_select_fusion.bm_ref, f32[64,256]{1,0:T(8,128)} %reshape.57.bar_ref.refs_8_), custom_call_target="tpu_custom_call" | custom-call | tf_op jit(solution)/shard_map/front/pallas_call | solution.py:412
  137.9 15.3 %assemble.1.s_ref = f32[1024,2048]{1,0:T(8,128)} custom-call(s32[512]{0:T(512)} %reshape.54.touched_ref, s32[64]{0:T(128)} %select_reduce_fusion.list_ref, s32[1]{0:T(128)} %bitcast.1.count_ref, bf16[64,256,256]{2,1,0:T(8,128)(2,1)} %bitcast.13, bf16[64,256,256]{2,1,0:T(8,128)(2,1)} %bitcast.14, bf16[64,256,256]{2,1,0:T(8,128)(2,1)} %bitcast.15, ...), custom_call_target="tpu_custom_call" | custom-call | tf_op jit(solution)/shard_map/assemble/pallas_call | solution.py:486
  153.2 62.8 %solve_panel.1 = (bf16[16,4,32,1024]{3,2,1,0:T(8,128)(2,1)}, bf16[8,4,32,1024]{3,2,1,0:T(8,128)(2,1)}, f32[8,16,8,256]{3,2,1,0:T(8,128)}) custom-call(f32[128,8,2048]{2,1,0:T(8,128)} %bitcast.21, f32[1024,1024]{1,0:T(8,128)} %get-tuple-element.13.w_hbm), custom_call_target="tpu_custom_call" | custom-call | tf_op jit(solution)/shard_map/solve_panel/pallas_call | solution.py:753
  216.0 10.3 %update.1 = f32[1024,2048]{1,0:T(8,128)} custom-call(f32[1024,2048]{1,0:T(8,128)} %assemble.1.s_ref, bf16[1024,1024]{1,0:T(8,128)(2,1)} %bitcast.23, bf16[2048,1024]{1,0:T(8,128)(2,1)} %bitcast.22, f32[1024,256]{1,0:T(8,128)} %bitcast.25), custom_call_target="tpu_custom_call" | custom-call | tf_op jit(solution)/shard_map/update/pallas_call | solution.py:807
